TPU v7x, 128 devices: a whole 4x4x4 slice. The times are simulated.
128 devices in a mesh: wide: 32 (over z, y, core), narrow: 4 (over x).
Axes of the slice: x: 4, y: 4, z: 4, core: 2. Of those that a mesh axis runs over, the one named last changes fastest.
Arguments:
- encoder_input: bfloat16 [32, 1024, 768], P('wide', 'narrow'), may hold values from -6 to 6
- seg_ids: int32 [32, 1024], P('wide'), may hold values from 0 to 6, as said below
- vis_slot: int32 [32, 1024], P('wide'), may hold values from 0 to 156, as said below
- restore_order: int32 [32, 4, 1568], P('wide', 'narrow'), may hold values from 0 to 1567, each once within a row
- enc_norm1_gain: bfloat16 [768], replicated, may hold values from 0.25 to 1.75
- enc_norm1_shift: bfloat16 [768], replicated, may hold values from -3 to 3
- enc_qkv_weight: bfloat16 [768, 2304], P('narrow'), may hold values from -0.21875 to 0.21875
- enc_qv_bias: bfloat16 [1536], replicated, may hold values from -3 to 3
- enc_proj_weight: bfloat16 [768, 768], P('narrow'), may hold values from -1.5 to 1.5
- enc_proj_bias: bfloat16 [768], replicated, may hold values from -3 to 3
- enc_norm2_gain: bfloat16 [768], replicated, may hold values from 0.25 to 1.75
- enc_norm2_shift: bfloat16 [768], replicated, may hold values from -3 to 3
- enc_fc1_weight: bfloat16 [768, 3072], P('narrow'), may hold values from -0.21875 to 0.21875
- enc_fc1_bias: bfloat16 [3072], replicated, may hold values from -3 to 3
- enc_fc2_weight: bfloat16 [3072, 768], P('narrow'), may hold values from -0.109375 to 0.109375
- enc_fc2_bias: bfloat16 [768], replicated, may hold values from -3 to 3
- to_dec_weight: bfloat16 [768, 384], replicated, may hold values from -0.21875 to 0.21875
- mask_token: bfloat16 [384], replicated, may hold values from -4 to 4
- dec_norm1_gain: bfloat16 [384], replicated, may hold values from 0.25 to 1.75
- dec_norm1_shift: bfloat16 [384], replicated, may hold values from -3 to 3
- dec_qkv_weight: bfloat16 [384, 1152], replicated, may hold values from -0.3125 to 0.3125
- dec_qv_bias: bfloat16 [768], replicated, may hold values from -3 to 3
- dec_proj_weight: bfloat16 [384, 384], replicated, may hold values from -6 to 6
- dec_proj_bias: bfloat16 [384], replicated, may hold values from -3 to 3
- dec_norm2_gain: bfloat16 [384], replicated, may hold values from 0.25 to 1.75
- dec_norm2_shift: bfloat16 [384], replicated, may hold values from -3 to 3
- dec_fc1_weight: bfloat16 [384, 1536], replicated, may hold values from -0.3125 to 0.3125
- dec_fc1_bias: bfloat16 [1536], replicated, may hold values from -3 to 3
- dec_fc2_weight: bfloat16 [1536, 384], replicated, may hold values from -0.15625 to 0.15625
- dec_fc2_bias: bfloat16 [384], replicated, may hold values from -3 to 3
- out_grad: bfloat16 [32, 4, 1568, 384], P('wide', 'narrow'), may hold values from -6 to 6
Outputs:
- dec_output: bfloat16 [32, 4, 1568, 384], P('wide', 'narrow')
- enc_input_grad: float32 [32, 1024, 768], P('wide', 'narrow')
- grad_enc_norm1_gain: float32 [768], replicated
- grad_enc_norm1_shift: float32 [768], replicated
- grad_enc_qkv_weight: float32 [768, 2304], replicated
- grad_enc_qv_bias: float32 [1536], replicated
- grad_enc_proj_weight: float32 [768, 768], replicated
- grad_enc_proj_bias: float32 [768], replicated
- grad_enc_norm2_gain: float32 [768], replicated
- grad_enc_norm2_shift: float32 [768], replicated
- grad_enc_fc1_weight: float32 [768, 3072], replicated
- grad_enc_fc1_bias: float32 [3072], replicated
- grad_enc_fc2_weight: float32 [3072, 768], replicated
- grad_enc_fc2_bias: float32 [768], replicated
- grad_to_dec_weight: float32 [768, 384], replicated
- grad_mask_token: float32 [384], replicated
- grad_dec_norm1_gain: float32 [384], replicated
- grad_dec_norm1_shift: float32 [384], replicated
- grad_dec_qkv_weight: float32 [384, 1152], replicated
- grad_dec_qv_bias: float32 [768], replicated
- grad_dec_proj_weight: float32 [384, 384], replicated
- grad_dec_proj_bias: float32 [384], replicated
- grad_dec_norm2_gain: float32 [384], replicated
- grad_dec_norm2_shift: float32 [384], replicated
- grad_dec_fc1_weight: float32 [384, 1536], replicated
- decoder_first_bias_grad: float32 [1536], replicated
- grad_dec_fc2_weight: float32 [1536, 384], replicated
- grad_dec_fc2_bias: float32 [384], replicated
Inputs may be any that keep to these rules, and one draw needn't show every extreme that they name: `seg_ids`: in each row every clip 0 to 5 has exactly 157 positions and the remaining positions carry 6 (padding); each index of narrow (positions k * 256 to (k + 1) * 256 - 1 of a row) holds between 1 and 64 tokens of every clip 0 to 3, and in every row some index holds exactly 64 of one of them. `vis_slot`: within a row, the positions of one clip carry the slots 0 to 156, each once; padding positions carry 0. `restore_order`: each clip's row holds every number of 0 to 1567 once.
All inputs are finite; a program needn't handle non-finite values.
Results may differ from a plain program's by a relative error of at most 0.018.
Values may be sent and summed in bfloat16 or wider, within the bound.
No kernel may reach another device: no remote copies, remote signals or barrier semaphores. Data moves between devices by JAX's collectives and lax.ppermute only.
A program may use at most 384 MiB of HBM per device.

v0:
```python
import functools

import jax
import jax.numpy as jnp
import numpy as np
from jax import lax
from jax.experimental import pallas as pl
from jax.experimental.pallas import tpu as pltpu
from jax.sharding import Mesh
from jax.sharding import PartitionSpec as P

HEADS = 12
DD = 384
DHEADS = 6
VIS = 157
FULL = 1568
CAP = 64
NORM_EPS = 1e-06
NEG_LARGE = -1e30
ALL = ("z", "y", "core", "x")
WIDE = ("z", "y", "core")
F32 = jnp.float32
BF16 = jnp.bfloat16


def room(mebibytes):
    return pltpu.CompilerParams(vmem_limit_bytes=mebibytes << 20)


def shift(value, axis, step):
    return lax.ppermute(value, axis, [(i, (i + step) % 4) for i in range(4)])


def swap(value):
    return lax.ppermute(value, "core", [(0, 1), (1, 0)])


def spread(piece, axis):
    across = shift(piece, axis, 2)
    return [piece, shift(piece, axis, 1), across, shift(piece, axis, 3)]


def exchange(pieces, axis, sign=1):
    far = shift(pieces[2], axis, 2)
    return [pieces[0], shift(pieces[1], axis, sign), far, shift(pieces[3], axis, -sign)]


def reduce_phase(current, axis):
    rows = current.shape[0] // 4
    index = lax.axis_index(axis)
    got = []
    for step in (2, 1, 3):
        piece = lax.dynamic_slice_in_dim(current, ((index + step) % 4) * rows, rows, 0)
        got.append(shift(piece.astype(BF16), axis, step).astype(F32))
    own = lax.dynamic_slice_in_dim(current, index * rows, rows, 0).astype(F32)
    return own + (got[0] + got[1] + got[2])


def sum_vector(vector):
    vector = vector + swap(vector)
    for axis in ("x", "y", "z"):
        parts = spread(vector, axis)
        vector = (parts[0] + parts[1]) + (parts[2] + parts[3])
    return vector


def pick(values, index):
    low = jnp.where(index == 0, values[0], values[1])
    high = jnp.where(index == 2, values[2], values[3])
    return jnp.where(index < 2, low, high)


def place_of(axes):
    return jnp.stack([lax.axis_index(a) for a in axes]).astype(jnp.int32)


def tail_kernel(place, *refs):
    ins, out, extra = refs[:8], refs[8], refs[9]
    half = pl.program_id(0)
    low = out.shape[0] // 4
    for b in range(4):
        rows = pl.ds(b * low, low)
        parts = [jnp.where(half == 0, ins[k][rows, :], ins[4 + k][rows, :]) for k in range(4)]
        parts = [pick(parts, (place[0] + 4 - g) % 4).astype(F32) for g in range(4)]
        to = pl.multiple_of(((place[2] + 4 - b) % 4) * low, 8)
        for c in range(3):
            out[pl.ds(to, low), c * 768 : (c + 1) * 768] = jnp.concatenate(
                [part[:, c * 192 : (c + 1) * 192] for part in parts], axis=1
            )
        extra[pl.ds(to, low), :] = jnp.concatenate([part[:, 576:] for part in parts], axis=1)


def tail_sum(own_half, other_half):
    current = own_half.astype(F32) + swap(other_half).astype(F32)
    current = reduce_phase(current, "y")
    current = reduce_phase(current, "z")
    parts = spread(current.astype(BF16), "z")
    parts = spread(jnp.concatenate(parts, 0), "y")
    mine = spread(jnp.concatenate(parts, 0), "x")
    theirs = [swap(part) for part in mine]
    rows, cols = mine[0].shape
    piece = pl.BlockSpec((rows // 4, cols), lambda h, a, s: (a, 0))
    return pl.pallas_call(
        tail_kernel,
        grid_spec=pltpu.PrefetchScalarGridSpec(
            num_scalar_prefetch=1,
            grid=(2, 4),
            in_specs=[piece] * 8,
            out_specs=[
                pl.BlockSpec(
                    (rows // 4, 4 * count),
                    lambda h, a, s: (((s[3] + h) % 2) * 4 + (s[1] + 4 - a) % 4, 0),
                )
                for count in (576, 64)
            ],
        ),
        out_shape=[jax.ShapeDtypeStruct((2 * rows, 4 * count), F32) for count in (576, 64)],
        compiler_params=room(16),
    )(place_of(("x", "y", "z", "core")), *mine, *theirs)


def dot_nt(left, right):
    return lax.dot_general(left, right, (((1,), (1,)), ((), ())), preferred_element_type=F32)


def dot_nn(left, right):
    return lax.dot_general(left, right, (((1,), (0,)), ((), ())), preferred_element_type=F32)


def low_lanes(rows):
    return lax.broadcasted_iota(jnp.int32, (rows, 128), 1) < 64


def two_heads(ref, at, count):
    pair = ref[pl.ds(at, count), :]
    low, zero = low_lanes(count), jnp.zeros_like(pair)
    return jnp.concatenate([jnp.where(low, pair, zero), jnp.where(low, zero, pair)], axis=0)


def mask_scores(scores, seg_q, seg_k, at, count):
    if seg_q is None:
        return scores
    mine = seg_q[pl.ds(at, count), :]
    allowed = jnp.concatenate([mine, mine], axis=0) == seg_k[...]
    return jnp.where(allowed, scores, NEG_LARGE)


def forward_kernel(*refs, block, masked):
    if masked:
        seg_q, seg_k, q_ref, k_ref, v_ref, out_ref, lse_ref = refs
    else:
        seg_q = seg_k = None
        q_ref, k_ref, v_ref, out_ref, lse_ref = refs
    count = q_ref.shape[0] // block
    low = low_lanes(block)

    def scores_of(i):
        scores = dot_nt(two_heads(q_ref, i * block, block), k_ref[...])
        return mask_scores(scores, seg_q, seg_k, i * block, block)

    scores = scores_of(0)
    for i in range(count):
        later = scores_of(i + 1) if i + 1 < count else None
        peak = jnp.max(scores, axis=1, keepdims=True)
        probs = jnp.exp(scores - peak)
        total = jnp.sum(probs, axis=1, keepdims=True)
        out = dot_nn(probs.astype(BF16), v_ref[...]) * (1.0 / total)
        rows = pl.ds(i * block, block)
        out_ref[rows, :] = jnp.where(low, out[:block], out[block:]).astype(BF16)
        lse = peak + jnp.log(total)
        lse_ref[0, rows, :] = jnp.concatenate([lse[:block], lse[block:]], axis=1)
        scores = later


def backward_kernel(*refs, block, masked, first):
    if masked:
        seg_q, seg_k = refs[:2]
        refs = refs[2:]
    else:
        seg_q = seg_k = None
    q_ref, k_ref, v_ref, out_ref, grad_ref, lse_ref = refs[:6]
    res_ref, k_sum, v_sum = refs[6 + first :]
    length = q_ref.shape[0]
    count = length // block
    low = low_lanes(block)
    pair = pl.program_id(0)
    width = res_ref.shape[1] // 3
    at_q = pl.multiple_of(pair * 128, 128)
    at_k = pl.multiple_of(width + pair * 128, 128)
    at_v = pl.multiple_of(2 * width + pair * 128, 128)

    def front(i):
        queries = two_heads(q_ref, i * block, block)
        grads = two_heads(grad_ref, i * block, block)
        scores = mask_scores(dot_nt(queries, k_ref[...]), seg_q, seg_k, i * block, block)
        return queries, grads, scores, dot_nt(grads, v_ref[...])

    current = front(0)
    for i in range(count):
        later = front(i + 1) if i + 1 < count else None
        queries, grads, scores, probs_grad = current
        rows = pl.ds(i * block, block)
        lse = lse_ref[0, rows, :]
        lse = jnp.concatenate([lse[:, 0:1], lse[:, 1:2]], axis=0)
        inner = grad_ref[rows, :].astype(F32) * out_ref[rows, :].astype(F32)
        zero = jnp.zeros_like(inner)
        inner = jnp.concatenate(
            [
                jnp.sum(jnp.where(low, inner, zero), axis=1, keepdims=True),
                jnp.sum(jnp.where(low, zero, inner), axis=1, keepdims=True),
            ],
            axis=0,
        )
        probs = jnp.exp(scores - lse)
        score_grad = (probs * (probs_grad - inner)).astype(BF16)
        q_grad = dot_nn(score_grad, k_ref[...])
        q_grad = jnp.where(low, q_grad[:block], q_grad[block:]).astype(BF16).astype(F32)
        res_ref[rows, pl.ds(at_q, 128)] = (q_grad * 0.125).astype(BF16)
        v_part = dot_nn(grads.T, probs.astype(BF16))
        k_part = dot_nn(queries.T, score_grad)
        if i == 0:
            k_sum[...] = k_part
            v_sum[...] = v_part
        else:
            k_sum[...] += k_part
            v_sum[...] += v_part
        current = later
    res_ref[:, pl.ds(at_k, 128)] = k_sum[...].T.astype(BF16)
    res_ref[:, pl.ds(at_v, 128)] = v_sum[...].T.astype(BF16)


def attention_specs(length, width, masked):
    pairs = width // 128
    column = lambda first: pl.BlockSpec((length, 128), lambda p: (0, first + p))
    segs = [
        pl.BlockSpec((length, 1), lambda p: (0, 0)),
        pl.BlockSpec((1, length), lambda p: (0, 0)),
    ]
    qkv = [column(0), column(pairs), column(2 * pairs)]
    stat = pl.BlockSpec((1, length, 2), lambda p: (p, 0, 0))
    return pairs, column, (segs if masked else []) + qkv, stat


def attend(qkv, segs, block):
    length, width = qkv.shape[0], qkv.shape[1] // 3
    masked = len(segs) > 0
    pairs, column, ins, stat = attention_specs(length, width, masked)
    work = 2 * pairs * length * length
    return pl.pallas_call(
        functools.partial(forward_kernel, block=block, masked=masked),
        grid=(pairs,),
        in_specs=ins,
        out_specs=[column(0), stat],
        out_shape=[
            jax.ShapeDtypeStruct((length, width), BF16),
            jax.ShapeDtypeStruct((pairs, length, 2), F32),
        ],
        compiler_params=room(26),
        cost_estimate=pl.CostEstimate(
            flops=work * 64 * 16, bytes_accessed=length * width * 8, transcendentals=work
        ),
    )(*segs, qkv, qkv, qkv)


def attend_back(qkv, out, grad, lse, segs, block, first=()):
    length, width = qkv.shape[0], qkv.shape[1] // 3
    masked = len(segs) > 0
    pairs, column, ins, stat = attention_specs(length, width, masked)
    work = 2 * pairs * length * length
    return pl.pallas_call(
        functools.partial(backward_kernel, block=block, masked=masked, first=len(first)),
        grid=(pairs,),
        in_specs=ins
        + [column(0), column(0), stat]
        + [pl.BlockSpec(memory_space=pl.ANY)] * len(first),
        out_specs=pl.BlockSpec((length, 3 * width), lambda p: (0, 0)),
        out_shape=jax.ShapeDtypeStruct((length, 3 * width), BF16),
        scratch_shapes=[pltpu.VMEM((128, length), F32)] * 2,
        compiler_params=room(27),
        cost_estimate=pl.CostEstimate(
            flops=work * 64 * 40, bytes_accessed=length * width * 16, transcendentals=work
        ),
    )(*segs, qkv, qkv, qkv, out, grad, lse, *first)


def sincos_table(count_pos, count_col):
    position = np.arange(count_pos).astype(np.float32)[:, None]
    column = np.arange(count_col)
    exponent = (2 * (column // 2)).astype(np.float32) / np.float32(count_col)
    angles = position / np.power(np.float32(10000.0), exponent)[None, :]
    table = np.where(column[None, :] % 2 == 0, np.sin(angles), np.cos(angles))
    return table.astype(np.float32)


def shape(rows, cols, dtype):
    return jax.ShapeDtypeStruct((rows, cols), dtype)


def cost(flops, moved, special=0):
    return pl.CostEstimate(flops=flops, bytes_accessed=moved, transcendentals=special)


def norm_parts(values):
    average = jnp.mean(values, axis=-1, keepdims=True)
    centred = values - average
    variance = jnp.mean(centred * centred, axis=-1, keepdims=True)
    inv_std = lax.rsqrt(variance + NORM_EPS)
    return centred * inv_std, inv_std


def norm_back(gradient, normed, inv_std, gain):
    scaled = gradient * gain
    return inv_std * (
        scaled
        - jnp.mean(scaled, axis=-1, keepdims=True)
        - normed * jnp.mean(scaled * normed, axis=-1, keepdims=True)
    )


def column_sum(values):
    return jnp.sum(values, axis=0, keepdims=True)


def mm_grad(left, right):
    return jnp.einsum("sk,sn->kn", left, right, preferred_element_type=F32)


def gelu_parts(u):
    cdf = 0.5 + 0.5 * lax.erf(u * 0.7071067811865476)
    bell = jnp.exp(u * u * -0.5)
    return u * cdf, cdf + u * (bell * 0.3989422804014327)


class Vectors:
    def __init__(self, arrays):
        self.at, self.size, total = {}, {}, 0
        for name, array in arrays.items():
            self.at[name], self.size[name] = total, array.shape[0]
            total += array.shape[0]
        self.total = total
        self.row = jnp.concatenate(list(arrays.values())).astype(F32).reshape(1, total)

    def of(self, ref, name, first=0, count=None):
        at = self.at[name] + first
        return ref[:, at : at + (self.size[name] - first if count is None else count)]


def group_kernel(place, weight, inputs, *outs):
    width = weight.shape[1] // 3
    part = width // 4
    rows = inputs.shape[0]
    for k in range(3):
        outs[1 + k][:rows, :] = inputs[...]
    for g in range(4):
        cols = []
        for c in range(3):
            cols.append(weight[:, c * width + g * part : c * width + (g + 1) * part])
            cols.append(jnp.zeros((weight.shape[0], 256 - part), BF16))
        piece = jnp.concatenate(cols, axis=1)

        @pl.when(place[0] == g)
        def _():
            outs[0][...] = piece

        half = piece.shape[0] // 2
        own = jnp.where(place[1] == 0, piece[:half], piece[half:])
        for k in range(1, 4):

            @pl.when((place[0] + k) % 4 == g)
            def _():
                outs[k][rows:, :] = own


def group_pieces(weight, inputs, place):
    rows, count = weight.shape[0], inputs.shape[0]
    outs = [shape(rows, 768, BF16)] + [shape(count + rows // 2, 768, BF16)] * 3
    whole = lambda a: pl.BlockSpec(a.shape, lambda i, s: (0, 0))
    return pl.pallas_call(
        group_kernel,
        grid_spec=pltpu.PrefetchScalarGridSpec(
            num_scalar_prefetch=1,
            grid=(1,),
            in_specs=[whole(weight), whole(inputs)],
            out_specs=[whole(a) for a in outs],
        ),
        out_shape=outs,
        compiler_params=room(10),
    )(place, weight, inputs)


def enc_in_kernel(place, *refs, vectors):
    own, piece, others, swapped, vec = refs[0], refs[1], refs[2:5], refs[5], refs[6]
    qkv_ref, low_ref, weight_ref = refs[7:]
    tokens, rows = own.shape[0], piece.shape[0]
    half = rows // 2
    weight_ref[pl.ds(pl.multiple_of(place[0] * rows, 16), rows), :] = piece[...]
    for k in range(1, 4):
        to = ((place[0] + 4 - k) % 4) * rows
        mine = pl.multiple_of(to + place[1] * half, 16)
        weight_ref[pl.ds(mine, half), :] = others[k - 1][tokens:, :]
        rest = pl.multiple_of(to + (1 - place[1]) * half, 16)
        weight_ref[pl.ds(rest, half), :] = swapped[(k - 1) * half : k * half, :]
    biases = []
    for first in (0, 768):
        groups = [vectors.of(vec, "enc_qv_bias", first + g * 192, 192) for g in range(4)]
        biases += [pick(groups, place[0]), jnp.zeros((1, 64), F32)]
    bias = jnp.concatenate(biases[:2] + [jnp.zeros((1, 256), F32)] + biases[2:], axis=1)
    scale = jnp.where(lax.broadcasted_iota(jnp.int32, (1, 768), 1) < 256, 0.125, 1.0)
    gain, offset = vectors.of(vec, "enc_norm1_gain"), vectors.of(vec, "enc_norm1_shift")
    for k in range(4):
        inputs = own[...] if k == 0 else others[k - 1][:tokens, :]
        normed, _ = norm_parts(inputs.astype(F32))
        low = (normed * gain + offset).astype(BF16)
        out = pl.ds(k * tokens, tokens)
        low_ref[out, :] = low
        qkv_ref[out, :] = ((dot_nn(low, weight_ref[...]) + bias) * scale).astype(BF16)


def enc_in(own, piece, others, swapped, vectors, place):
    tokens, width = own.shape
    rows = 4 * tokens
    whole = lambda a: pl.BlockSpec(a.shape, lambda i, s: (0, 0))
    outs = [shape(rows, 768, BF16), shape(rows, width, BF16), shape(width, 768, BF16)]
    return pl.pallas_call(
        functools.partial(enc_in_kernel, vectors=vectors),
        grid_spec=pltpu.PrefetchScalarGridSpec(
            num_scalar_prefetch=1,
            grid=(1,),
            in_specs=[whole(a) for a in (own, piece, *others, swapped, vectors.row)],
            out_specs=[whole(a) for a in outs],
        ),
        out_shape=outs,
        compiler_params=room(20),
        cost_estimate=cost(2 * rows * width * 768, rows * width * 8),
    )(place, own, piece, *others, swapped, vectors.row)


MATRIX_SPECS = [
    pl.BlockSpec((1, 768, 768), lambda j, s: (4, 0, 0)),
    pl.BlockSpec((1, 768, 768), lambda j, s: (5 + j, 0, 0)),
    pl.BlockSpec((4, 192, 768), lambda j, s: (0, j, 0)),
]


def enc_block_kernel(place, *refs, vectors):
    parts, (x, proj, fc1, fc2, to_dec, send_map, vec) = refs[:4], refs[4:11]
    att_ref, x1_ref, low_ref, act_ref, slope_ref, y_ref, *sends, total = refs[11:]
    step = pl.program_id(0)

    @pl.when(step == 0)
    def _():
        groups = [part[...] for part in parts]
        att = jnp.concatenate([pick(groups, (place[0] + 4 - g) % 4) for g in range(4)], axis=1)
        att_ref[...] = att
        x1 = x[...].astype(F32) + (dot_nn(att, proj[0]) + vectors.of(vec, "enc_proj_bias"))
        x1_ref[...] = x1
        normed, _ = norm_parts(x1)
        gain, offset = vectors.of(vec, "enc_norm2_gain"), vectors.of(vec, "enc_norm2_shift")
        low_ref[...] = (normed * gain + offset).astype(BF16)
        total[...] = x1 + vectors.of(vec, "enc_fc2_bias")

    bias = pick([vectors.of(vec, "enc_fc1_bias", j * 768, 768) for j in range(4)], step)
    pre = dot_nn(low_ref[...], fc1[0]) + bias
    act, slope = gelu_parts(pre)
    act = act.astype(BF16)
    act_ref[...] = act
    slope_ref[...] = slope.astype(BF16)
    total[...] += dot_nn(act, fc2[...].reshape(768, 768))

    @pl.when(step == 3)
    def _():
        y = total[...].astype(BF16)
        y_ref[...] = y
        reduced = dot_nn(y, to_dec[...]).astype(BF16)
        send = dot_nn(send_map[...], reduced).astype(BF16)
        for k in range(4):
            sends[k][...] = send[k * CAP : (k + 1) * CAP, :]


def enc_block(parts, x, matrices, to_dec, send_map, vectors, place):
    rows, width = x.shape
    whole = lambda a: pl.BlockSpec(a.shape, lambda j, s: (0,) * len(a.shape))
    chunk = pl.BlockSpec((rows, 768), lambda j, s: (0, j))
    outs = [
        shape(rows, width, BF16),
        shape(rows, width, F32),
        shape(rows, width, BF16),
        shape(rows, 4 * width, BF16),
        shape(rows, 4 * width, BF16),
        shape(rows, width, BF16),
        *[shape(CAP, DD, BF16)] * 4,
    ]
    return pl.pallas_call(
        functools.partial(enc_block_kernel, vectors=vectors),
        grid_spec=pltpu.PrefetchScalarGridSpec(
            num_scalar_prefetch=1,
            grid=(4,),
            in_specs=[whole(a) for a in (*parts, x)]
            + MATRIX_SPECS
            + [whole(a) for a in (to_dec, send_map, vectors.row)],
            out_specs=[
                chunk if a.shape[-1] == 4 * width else whole(a) for a in outs
            ],
            scratch_shapes=[pltpu.VMEM((rows, width), F32)],
        ),
        out_shape=outs,
        compiler_params=room(18),
        cost_estimate=cost(rows * width * width * 20, width * width * 20, rows * width * 8),
    )(place, *parts, x, *[matrices] * 3, to_dec, send_map, vectors.row)


def enc_block_back_kernel(place, *refs, vectors, first):
    parts, (send_map, to_dec, x1, y, low, att) = refs[:4], refs[4:10]
    act, slope, proj, fc1, fc2, vec = refs[10:16]
    refs = refs[16 + first :]
    fc1_g, fc2_g, fc1_b, gx1_ref, proj_g, to_dec_g = refs[:6]
    gatt_refs, (fc2_b, gain_g, shift_g, proj_b) = refs[6:10], refs[10:14]
    gz, gy, back, low_turned = refs[14:]
    step = pl.program_id(0)

    @pl.when(step == 0)
    def _():
        rows = jnp.concatenate([part[...] for part in parts], axis=0)
        reduced = dot_nn(send_map[...], rows).astype(BF16)
        to_dec_g[...] = dot_nn(y[...].T, reduced).astype(BF16)
        grad = dot_nt(reduced, to_dec[...])
        gy[...] = grad
        gz[...] = grad.astype(BF16)
        fc2_b[...] = column_sum(grad.astype(BF16).astype(F32))
        back[...] = jnp.zeros_like(back)
        low_turned[...] = low[...].T

    fc2_g[...] = dot_nn(act[...].T, gz[...]).astype(BF16)
    gpre = dot_nt(gz[...], fc2[...].reshape(768, 768)) * slope[...].astype(F32)
    gpre = gpre.astype(BF16)
    fc1_b[...] = column_sum(gpre.astype(F32))
    fc1_g[...] = dot_nn(low_turned[...], gpre).astype(BF16)
    back[...] += dot_nt(gpre, fc1[0])

    @pl.when(step == 3)
    def _():
        normed, inv_std = norm_parts(x1[...])
        total = back[...]
        gain_g[...] = column_sum(total * normed)
        shift_g[...] = column_sum(total)
        gx1 = gy[...] + norm_back(total, normed, inv_std, vectors.of(vec, "enc_norm2_gain"))
        gx1_ref[...] = gx1
        go = gx1.astype(BF16)
        proj_b[...] = column_sum(go.astype(F32))
        proj_g[...] = dot_nn(att[...].T, go).astype(BF16)
        gatt = dot_nt(go, proj[0]).astype(BF16)
        groups = [gatt[:, g * 192 : (g + 1) * 192] for g in range(4)]
        for k in range(4):
            gatt_refs[k][...] = pick(groups, (place[0] + k) % 4)


def enc_block_back(
    parts, send_map, to_dec, x1, y, low, att, act, slope, matrices, vectors, place, first
):
    rows, width = x1.shape
    whole = lambda a: pl.BlockSpec(a.shape, lambda j, s: (0,) * len(a.shape))
    columns = lambda count: pl.BlockSpec((count, 768), lambda j, s: (0, j))
    rest = [
        shape(rows, width, F32),
        shape(width, width, BF16),
        shape(width, DD, BF16),
        *[shape(rows, 192, BF16)] * 4,
        *[shape(1, width, F32)] * 4,
    ]
    return pl.pallas_call(
        functools.partial(enc_block_back_kernel, vectors=vectors, first=len(first)),
        grid_spec=pltpu.PrefetchScalarGridSpec(
            num_scalar_prefetch=1,
            grid=(4,),
            in_specs=[whole(a) for a in (*parts, send_map, to_dec, x1, y, low, att)]
            + [columns(rows), columns(rows), *MATRIX_SPECS, whole(vectors.row)]
            + [pl.BlockSpec(memory_space=pl.ANY)] * len(first),
            out_specs=[
                columns(width),
                pl.BlockSpec((768, width), lambda j, s: (j, 0)),
                columns(1),
            ]
            + [whole(a) for a in rest],
            scratch_shapes=[
                pltpu.VMEM((rows, width), BF16),
                pltpu.VMEM((rows, width), F32),
                pltpu.VMEM((rows, width), F32),
                pltpu.VMEM((width, rows), BF16),
            ],
        ),
        out_shape=[
            shape(width, 4 * width, BF16),
            shape(4 * width, width, BF16),
            shape(1, 4 * width, F32),
            *rest,
        ],
        compiler_params=room(32),
        cost_estimate=cost(rows * width * width * 40, width * width * 40),
    )(
        place,
        *parts,
        send_map,
        to_dec,
        x1,
        y,
        low,
        att,
        act,
        slope,
        *[matrices] * 3,
        vectors.row,
        *first,
    )


def enc_in_back_kernel(*refs, vectors):
    inputs, (grad, weight, vec) = refs[:4], refs[4:7]
    own_ref, others, (gain_g, shift_g, grad_sum) = refs[7], refs[8:11], refs[11:]
    tokens = inputs[0].shape[0]
    gains = shifts = 0.0
    for k in range(4):
        part = dot_nt(grad[pl.ds(k * tokens, tokens), :], weight[...])
        normed, _ = norm_parts(inputs[k][:tokens, :].astype(F32))
        gains = gains + column_sum(part * normed)
        shifts = shifts + column_sum(part)
        if k == 0:
            own_ref[...] = part
        else:
            others[k - 1][...] = part.astype(BF16)
    gain_g[...] = gains
    shift_g[...] = shifts
    grad_sum[...] = column_sum(grad[...].astype(F32))


def enc_in_back(inputs, grad, weight, vectors):
    tokens, width = inputs[0].shape
    outs = [shape(tokens, width, F32)] + [shape(tokens, width, BF16)] * 3
    outs += [shape(1, width, F32)] * 2 + [shape(1, 768, F32)]
    return pl.pallas_call(
        functools.partial(enc_in_back_kernel, vectors=vectors),
        out_shape=outs,
        compiler_params=room(14),
        cost_estimate=cost(8 * tokens * width * 768, tokens * width * 32),
    )(*inputs, grad, weight, vectors.row)


def enc_end_kernel(x, gx1, own, a, b, c, vec, out, *, vectors):
    normed, inv_std = norm_parts(x[...].astype(F32))
    back = own[...] + (a[...].astype(F32) + b[...].astype(F32) + c[...].astype(F32))
    out[...] = gx1[...] + norm_back(back, normed, inv_std, vectors.of(vec, "enc_norm1_gain"))


def enc_end(x, gx1, back, vectors):
    return pl.pallas_call(
        functools.partial(enc_end_kernel, vectors=vectors),
        out_shape=shape(*x.shape, F32),
        compiler_params=room(8),
    )(x, gx1, *back, vectors.row)


def dec_in_kernel(*refs, vectors):
    parts, (restore, slots, table, weight, vec) = refs[:4], refs[4:9]
    grid_ref, low_ref, qkv_ref = refs[9:]
    rows = jnp.concatenate([part[...] for part in parts], axis=0)
    order = restore[...]
    hot = jnp.where(order == slots[...], 1.0, 0.0).astype(BF16)
    placed = dot_nn(hot, rows)
    grid = placed + jnp.where(order >= VIS, vectors.of(vec, "mask_token"), 0.0) + table[...]
    grid_ref[...] = grid
    normed, _ = norm_parts(grid)
    low = normed * vectors.of(vec, "dec_norm1_gain") + vectors.of(vec, "dec_norm1_shift")
    low = low.astype(BF16)
    low_ref[...] = low
    packed = dot_nn(low, weight[...])
    queries = packed[:, :DD] + vectors.of(vec, "dec_qv_bias", 0, DD)
    qkv_ref[:, :DD] = (queries * 0.125).astype(BF16)
    qkv_ref[:, DD : 2 * DD] = packed[:, DD : 2 * DD].astype(BF16)
    values = packed[:, 2 * DD :] + vectors.of(vec, "dec_qv_bias", DD, DD)
    qkv_ref[:, 2 * DD :] = values.astype(BF16)


def dec_in(parts, restore, slots, table, weight, vectors, tile):
    rows = table.shape[0]
    row = lambda n: pl.BlockSpec((tile, n), lambda i: (i, 0))
    whole = lambda a: pl.BlockSpec(a.shape, lambda i: (0, 0))
    return pl.pallas_call(
        functools.partial(dec_in_kernel, vectors=vectors),
        grid=(rows // tile,),
        in_specs=[whole(a) for a in parts]
        + [row(1), whole(slots), row(DD), whole(weight), whole(vectors.row)],
        out_specs=[row(DD), row(DD), row(3 * DD)],
        out_shape=[shape(rows, DD, F32), shape(rows, DD, BF16), shape(rows, 3 * DD, BF16)],
        compiler_params=room(24),
        cost_estimate=cost(rows * DD * DD * 8, rows * DD * 16),
    )(*parts, restore, slots, table, weight, vectors.row)


def dec_in_back_kernel(grad, weight, grid, gx1, restore, column, slots, vec, *outs, vectors):
    slot_refs, (gain_g, shift_g, mask_g, grad_sum, total) = outs[:4], outs[4:]
    step = pl.program_id(0)

    @pl.when(step == 0)
    def _():
        for ref in (gain_g, shift_g, mask_g, grad_sum, total):
            ref[...] = jnp.zeros_like(ref)

    back = dot_nt(grad[...], weight[...])
    normed, inv_std = norm_parts(grid[...])
    gain_g[...] += column_sum(back * normed)
    shift_g[...] += column_sum(back)
    grad_sum[...] += column_sum(grad[...].astype(F32))
    gx = gx1[...] + norm_back(back, normed, inv_std, vectors.of(vec, "dec_norm1_gain"))
    order = restore[0]
    hot = jnp.where(slots[...] == order, 1.0, 0.0).astype(BF16)
    total[...] += dot_nn(hot, gx.astype(BF16))
    mask_g[...] += column_sum(jnp.where(column[...] >= VIS, gx, 0.0))

    @pl.when(step == pl.num_programs(0) - 1)
    def _():
        for k in range(4):
            slot_refs[k][...] = total[k * CAP : (k + 1) * CAP, :].astype(BF16)


def dec_in_back(grad, weight, grid, gx1, restore, column, slots, vectors, tile):
    rows = grid.shape[0]
    row = lambda n: pl.BlockSpec((tile, n), lambda i: (i, 0))
    whole = lambda shape: pl.BlockSpec(shape, lambda i: (0, 0))
    sums = [DD, DD, DD, 3 * DD]
    return pl.pallas_call(
        functools.partial(dec_in_back_kernel, vectors=vectors),
        grid=(rows // tile,),
        in_specs=[
            row(3 * DD),
            whole(weight.shape),
            row(DD),
            row(DD),
            pl.BlockSpec((1, 1, tile), lambda i: (i, 0, 0)),
            row(1),
            whole(slots.shape),
            whole(vectors.row.shape),
        ],
        out_specs=[whole((CAP, DD))] * 4 + [whole((1, n)) for n in sums],
        out_shape=[shape(CAP, DD, BF16)] * 4 + [shape(1, n, F32) for n in sums],
        scratch_shapes=[pltpu.VMEM((4 * CAP, DD), F32)],
        compiler_params=room(16),
        cost_estimate=cost(rows * DD * DD * 8, rows * DD * 16),
    )(grad, weight, grid, gx1, restore, column, slots, vectors.row)


def dec_mid_kernel(x, att, gy, proj, fc1, fc2, vec, *outs, vectors, chunk):
    y_ref, gx1_ref, go_ref, gatt_ref, fc1_g, fc2_g = outs[:6]
    (fc1_b, fc2_b, gain_g, shift_g, proj_b), (act_ref, slope, fc1_sum, fc2_sum) = (
        outs[6:11],
        outs[11:],
    )
    step = pl.program_id(0)

    @pl.when(step == 0)
    def _():
        for ref in (fc1_b, fc2_b, gain_g, shift_g, proj_b, fc1_sum, fc2_sum):
            ref[...] = jnp.zeros_like(ref)

    hidden = fc1.shape[1]
    gain = vectors.of(vec, "dec_norm2_gain")
    x1 = x[...] + (dot_nn(att[...], proj[...]) + vectors.of(vec, "dec_proj_bias"))
    normed, inv_std = norm_parts(x1)
    low = (normed * gain + vectors.of(vec, "dec_norm2_shift")).astype(BF16)
    total = x1 + vectors.of(vec, "dec_fc2_bias")

    def pre_of(c):
        return dot_nn(low, fc1[:, c : c + chunk]) + vectors.of(vec, "dec_fc1_bias", c, chunk)

    pre = pre_of(0)
    for c in range(0, hidden, chunk):
        later = pre_of(c + chunk) if c + chunk < hidden else None
        act, rise = gelu_parts(pre)
        act = act.astype(BF16)
        act_ref[:, c : c + chunk] = act
        slope[:, c : c + chunk] = rise.astype(BF16)
        total = total + dot_nn(act, fc2[c : c + chunk, :])
        pre = later
    y_ref[...] = total.astype(BF16)

    gz = gy[...]
    gz_turned = gz.T
    low_turned = low.T
    fc2_b[...] += column_sum(gz.astype(F32))
    grad = dot_nt(gz, fc2[:chunk, :])
    back = None
    for c in range(0, hidden, chunk):
        later = None
        if c + chunk < hidden:
            later = dot_nt(gz, fc2[c + chunk : c + 2 * chunk, :])
        fc2_sum[:, c : c + chunk] += dot_nn(gz_turned, act_ref[:, c : c + chunk])
        gpre = (grad * slope[:, c : c + chunk].astype(F32)).astype(BF16)
        fc1_b[:, c : c + chunk] += column_sum(gpre.astype(F32))
        fc1_sum[:, c : c + chunk] += dot_nn(low_turned, gpre)
        part = dot_nt(gpre, fc1[:, c : c + chunk])
        back = part if back is None else back + part
        grad = later
    gain_g[...] += column_sum(back * normed)
    shift_g[...] += column_sum(back)
    gx1 = gz.astype(F32) + norm_back(back, normed, inv_std, gain)
    gx1_ref[...] = gx1
    go = gx1.astype(BF16)
    go_ref[...] = go
    proj_b[...] += column_sum(go.astype(F32))
    gatt_ref[...] = dot_nt(go, proj[...]).astype(BF16)

    @pl.when(step == pl.num_programs(0) - 1)
    def _():
        fc1_g[...] = fc1_sum[...].astype(BF16)
        for c in range(0, hidden, chunk):
            fc2_g[c : c + chunk, :] = fc2_sum[:, c : c + chunk].T.astype(BF16)


def dec_mid(x, att, gy, proj, fc1, fc2, vectors, tile, chunk):
    rows, width = x.shape
    hidden = fc1.shape[1]
    row = lambda n: pl.BlockSpec((tile, n), lambda i: (i, 0))
    whole = lambda shape: pl.BlockSpec(shape, lambda i: (0, 0))
    consts = (proj, fc1, fc2, vectors.row)
    shapes = [(width, BF16), (width, F32), (width, BF16), (width, BF16)]
    fixed = [shape(width, hidden, BF16), shape(hidden, width, BF16)]
    fixed += [shape(1, n, F32) for n in (hidden, width, width, width, width)]
    return pl.pallas_call(
        functools.partial(dec_mid_kernel, vectors=vectors, chunk=chunk),
        grid=(rows // tile,),
        in_specs=[row(width)] * 3 + [whole(a.shape) for a in consts],
        out_specs=[row(n) for n, _ in shapes] + [whole(a.shape) for a in fixed],
        out_shape=[shape(rows, n, t) for n, t in shapes] + fixed,
        scratch_shapes=[pltpu.VMEM((tile, hidden), BF16)] * 2
        + [pltpu.VMEM((width, hidden), F32)] * 2,
        compiler_params=room(42),
        cost_estimate=cost(rows * hidden * width * 28, rows * width * 20, rows * hidden * 2),
    )(x, att, gy, *consts)


def widen_kernel(*refs):
    count = len(refs) // 2
    for k in range(count):
        refs[count + k][...] = refs[k][...].astype(F32)


def widen(arrays):
    piece = lambda a: pl.BlockSpec((a.shape[0] // 8, a.shape[1]), lambda i: (i, 0))
    return pl.pallas_call(
        widen_kernel,
        grid=(8,),
        in_specs=[piece(a) for a in arrays],
        out_specs=[piece(a) for a in arrays],
        out_shape=[shape(*a.shape, F32) for a in arrays],
        compiler_params=room(16),
        cost_estimate=cost(0, sum(a.shape[0] * a.shape[1] * 6 for a in arrays)),
    )(*arrays)


def body(
    encoder_input,
    seg_ids,
    vis_slot,
    restore_order,
    enc_norm1_gain,
    enc_norm1_shift,
    enc_qkv_weight,
    enc_qv_bias,
    enc_proj_weight,
    enc_proj_bias,
    enc_norm2_gain,
    enc_norm2_shift,
    enc_fc1_weight,
    enc_fc1_bias,
    enc_fc2_weight,
    enc_fc2_bias,
    to_dec_weight,
    mask_token,
    dec_norm1_gain,
    dec_norm1_shift,
    dec_qkv_weight,
    dec_qv_bias,
    dec_proj_weight,
    dec_proj_bias,
    dec_norm2_gain,
    dec_norm2_shift,
    dec_fc1_weight,
    dec_fc1_bias,
    dec_fc2_weight,
    dec_fc2_bias,
    out_grad,
):
    x_at = lax.axis_index("x")
    core = lax.axis_index("core")
    place = place_of(("x", "core"))
    tokens, width = encoder_input.shape[1:]
    hw = width // 4
    vectors = Vectors(
        {
            "enc_norm1_gain": enc_norm1_gain,
            "enc_norm1_shift": enc_norm1_shift,
            "enc_qv_bias": enc_qv_bias,
            "enc_proj_bias": enc_proj_bias,
            "enc_norm2_gain": enc_norm2_gain,
            "enc_norm2_shift": enc_norm2_shift,
            "enc_fc1_bias": enc_fc1_bias,
            "enc_fc2_bias": enc_fc2_bias,
            "mask_token": mask_token,
            "dec_norm1_gain": dec_norm1_gain,
            "dec_norm1_shift": dec_norm1_shift,
            "dec_qv_bias": dec_qv_bias,
            "dec_proj_bias": dec_proj_bias,
            "dec_norm2_gain": dec_norm2_gain,
            "dec_norm2_shift": dec_norm2_shift,
            "dec_fc1_bias": dec_fc1_bias,
            "dec_fc2_bias": dec_fc2_bias,
        }
    )

    own_input = encoder_input[0]
    piece, *others = exchange(group_pieces(enc_qkv_weight, own_input, place), "x")
    swapped = swap(jnp.concatenate([other[tokens:] for other in others], axis=0))
    inputs = [own_input, *others]

    eighth = hw // 8
    first_row = (core * 4 + lax.axis_index("y")) * eighth
    rows_of = lambda stack: lax.dynamic_slice_in_dim(stack, first_row, eighth, 1)
    strip = [
        rows_of(enc_fc2_weight.reshape(4, hw, width)),
        rows_of(enc_proj_weight[None]),
    ]
    fc1_rows = lax.dynamic_slice_in_dim(enc_fc1_weight, first_row, eighth, 0)
    strip += [fc1_rows[None, :, k * width : (k + 1) * width] for k in range(4)]
    matrices = lax.all_gather(
        jnp.concatenate(strip, axis=0), ("x", "core", "y"), axis=1, tiled=True
    )

    row_seg = seg_ids[0].reshape(4, tokens)
    row_slot = vis_slot[0].reshape(4, tokens)
    position = jnp.arange(tokens)
    earlier = position[None, :] < position[:, None]
    same_clip = row_seg[:, :, None] == row_seg[:, None, :]
    ranks = jnp.sum(jnp.logical_and(same_clip, earlier), axis=-1)
    turn = (x_at - jnp.arange(4)) % 4
    seg_turned = jnp.take(row_seg, turn, axis=0)
    segs = (seg_turned.reshape(4 * tokens, 1), seg_turned.reshape(1, 4 * tokens))
    own_seg = lax.dynamic_index_in_dim(row_seg, x_at, 0, keepdims=False)
    own_rank = lax.dynamic_index_in_dim(ranks, x_at, 0, keepdims=False)
    cap_index = jnp.arange(4 * CAP)
    clip_to = (x_at + cap_index // CAP) % 4
    send_map = jnp.logical_and(
        own_seg[None, :] == clip_to[:, None],
        own_rank[None, :] == (cap_index % CAP)[:, None],
    ).astype(BF16)
    send_back = jnp.logical_and(
        own_seg[:, None] == clip_to[None, :],
        own_rank[:, None] == (cap_index % CAP)[None, :],
    ).astype(BF16)
    chosen = jnp.logical_and(
        seg_turned[:, None, :] == x_at,
        jnp.take(ranks, turn, axis=0)[:, None, :] == jnp.arange(CAP)[None, :, None],
    )
    slot_turned = jnp.take(row_slot, turn, axis=0)
    slot_vis = jnp.sum(jnp.where(chosen, slot_turned[:, None, :] + 1, 0), axis=-1) - 1
    restore_row = restore_order[0, 0]
    restore_col = restore_row[:, None]
    restore_row = restore_row.reshape(2, 1, FULL // 2)
    table = jnp.asarray(sincos_table(FULL, DD))

    qkv, first_in, qkv_mine = enc_in(own_input, piece, others, swapped, vectors, place)
    att_mine, enc_lse = attend(qkv, segs, 128)
    blocks = att_mine.reshape(4, tokens, 256)
    parts = exchange([blocks[(4 - k) % 4, :, :hw] for k in range(4)], "x")
    attended, enc_x1, second_in, enc_act, enc_slope, enc_low, *sends = enc_block(
        parts, own_input, matrices, to_dec_weight, send_map, vectors, place
    )

    received = exchange(sends, "x")
    grid, dec_in_low, dec_qkv = dec_in(
        received,
        restore_col,
        slot_vis.reshape(1, 4 * CAP),
        table,
        dec_qkv_weight,
        vectors,
        FULL // 2,
    )
    dec_att, dec_lse = attend(dec_qkv, (), 224)

    dec_gz = out_grad[0, 0]
    dec_out, dec_gx1, dec_go, dec_gatt, dec_fc1_g, dec_fc2_g, *dec_sums = dec_mid(
        grid,
        dec_att,
        dec_gz,
        dec_proj_weight,
        dec_fc1_weight,
        dec_fc2_weight,
        vectors,
        FULL // 2,
        512,
    )
    dec_fc1_b, dec_fc2_b, dec_gain2_g, dec_shift2_g, dec_proj_b = dec_sums
    dec_gqkv = attend_back(dec_qkv, dec_att, dec_gatt, dec_lse, (), 112)
    *slot_grads, dec_gain1_g, dec_shift1_g, mask_g, dec_gqkv_sum = dec_in_back(
        dec_gqkv,
        dec_qkv_weight,
        grid,
        dec_gx1,
        restore_row,
        restore_col,
        slot_vis.reshape(4 * CAP, 1),
        vectors,
        FULL // 2,
    )
    slot_grads, dec_in_low, dec_att = lax.optimization_barrier((slot_grads, dec_in_low, dec_att))
    low_grad = lambda left, right: mm_grad(left, right).astype(BF16)
    dec_early = (low_grad(dec_in_low, dec_gqkv), low_grad(dec_att, dec_go), dec_fc1_g, dec_fc2_g)

    returned = exchange(slot_grads, "x", -1)
    enc_fc1_g, enc_fc2_g, enc_fc1_b, enc_gx1, enc_proj_g, to_dec_g, *rest = enc_block_back(
        returned,
        send_back,
        to_dec_weight,
        enc_x1,
        enc_low,
        second_in,
        attended,
        enc_act,
        enc_slope,
        matrices,
        vectors,
        place,
        dec_early[:2],
    )
    gatt_parts, (enc_fc2_b, enc_gain2_g, enc_shift2_g, enc_proj_b) = rest[:4], rest[4:]
    columns = lambda array, which: lax.dynamic_slice_in_dim(
        array, which * (array.shape[1] // 2), array.shape[1] // 2, 1
    )

    def halves(make):
        return make(core), make(1 - core)

    early = (*dec_early, enc_proj_g, enc_fc1_g, enc_fc2_g, to_dec_g)
    gatt_mine = jnp.concatenate(exchange(gatt_parts, "x"), axis=0)
    gatt_mine = jnp.pad(gatt_mine, ((0, 0), (0, 64)))
    def finish():
        gqkv = attend_back(qkv, att_mine, gatt_mine, enc_lse, segs, 128, early)
        own_back, *others, gain1_g, shift1_g, gqkv_sum = enc_in_back(
            inputs, gqkv, qkv_mine, vectors
        )

        qv = jnp.zeros((2, 4, hw), F32)
        qv = lax.dynamic_update_index_in_dim(
            qv, jnp.stack([gqkv_sum[0, :hw], gqkv_sum[0, 512 : 512 + hw]]), x_at, 1
        )
        small = [
            gain1_g,
            shift1_g,
            qv.reshape(1, 2 * width),
            enc_proj_b,
            enc_gain2_g,
            enc_shift2_g,
            enc_fc1_b,
            enc_fc2_b,
            mask_g,
            dec_gain1_g,
            dec_shift1_g,
            dec_gqkv_sum[:, :DD],
            dec_gqkv_sum[:, 2 * DD :],
            dec_proj_b,
            dec_gain2_g,
            dec_shift2_g,
            dec_fc1_b,
            dec_fc2_b,
        ]
        sizes = [v.shape[1] for v in small]
        vector = jnp.concatenate([*small, jnp.zeros((1, 14336 - sum(sizes)), F32)], axis=1)
        terms = spread(vector.reshape(112, 128), "x")
        vector = ((terms[0] + terms[1]) + (terms[2] + terms[3])).reshape(4, 56, 64)
        extra = lax.dynamic_index_in_dim(vector, x_at, 0, keepdims=False).astype(BF16)
        extra = jnp.pad(extra, ((0, width - 56), (0, 0)))

        def qkv_half(which):
            grad = low_grad(columns(first_in, which), gqkv)
            grad = [grad[:, c * 256 : c * 256 + hw] for c in range(3)]
            more = lax.dynamic_slice_in_dim(extra, which * (width // 2), width // 2, 0)
            return jnp.concatenate([*grad, more], axis=1)


        qkv_sum, vec_sum = tail_sum(*halves(qkv_half))
        back = exchange([None, *others], "x", -1)
        gx = enc_end(own_input, enc_gx1, (own_back, *back[1:]), vectors)
        return qkv_sum, vec_sum, gx

    def nothing():
        return tuple(
            jnp.zeros(dims, F32)
            for dims in ((width, 3 * width), (width, 256), (tokens, width))
        )

    rest_grads = lax.psum(early, ALL)
    qkv_grad, vector, input_grad = lax.cond(seg_ids[0, 0] >= 0, finish, nothing)
    vector = vector[:56].reshape(56, 4, 64).transpose(1, 0, 2).reshape(14336)
    sizes = [width, width, 2 * width, width, width, width, 4 * width, width, DD]
    sizes += [DD, DD, 2 * DD, DD, DD, DD, 4 * DD, DD]
    cuts = [int(c) for c in np.cumsum(sizes)]
    v = jnp.split(vector, cuts)

    dec_qkv_g, dec_proj_g, dec_fc1_g, dec_fc2_g, *rest_grads = widen(rest_grads)
    enc_proj_g, enc_fc1_g, enc_fc2_g, to_dec_g = rest_grads
    return (
        dec_out[None, None],
        input_grad[None],
        v[0],
        v[1],
        qkv_grad,
        v[2],
        enc_proj_g,
        v[3],
        v[4],
        v[5],
        enc_fc1_g,
        v[6],
        enc_fc2_g,
        v[7],
        to_dec_g,
        v[8],
        v[9],
        v[10],
        dec_qkv_g,
        v[11],
        dec_proj_g,
        v[12],
        v[13],
        v[14],
        dec_fc1_g,
        v[15],
        dec_fc2_g,
        v[16],
    )


def solution(mesh):
    fine = Mesh(mesh.devices.reshape(4, 4, 2, 4), ALL)
    row, shared, split = P(WIDE, None), P(), P("x", None)
    return jax.shard_map(
        body,
        mesh=fine,
        in_specs=(
            P(WIDE, "x", None),
            row,
            row,
            P(WIDE, "x", None),
            shared,
            shared,
            split,
            shared,
            split,
            shared,
            shared,
            shared,
            split,
            shared,
            split,
        )
        + (shared,) * 15
        + (P(WIDE, "x", None, None),),
        out_specs=(P(WIDE, "x", None, None), P(WIDE, "x", None)) + (shared,) * 26,
        check_vma=False,
    )
```

profile of v0, /device:TPU:1, one launch (start us, length us, event | category | flops | bytes accessed | tf_op | source)
XLA Modules:
  0.0 449.6 jit_solution(873582962855106427)
XLA Ops:
  13.3 2.1 shard_map.519
  15.4 2.1 collective-permute-start.26
  17.5 2.5 collective-permute-start.27
  26.0 4.4 collective-permute-done.26.refs_2_
  31.4 17.3 %collective-permute-done.27.refs_3_ = bf16[352,768]{1,0:T(8,128)(2,1)} collective-permute-done((bf16[352,768]{1,0:T(8,128)(2,1)S(1)}, bf16[352,768]{1,0:T(8,128)(2,1)}, u32[]{:S(2)}, u32[]{:S(2)}) %collective-permute-start.27) | collective-permute-done | bytes 540704 | tf_op jit(solution)/shard_map/ppermute | solution.py:31
  53.7 4.7 %shard_map.520 = (bf16[1024,768]{1,0:T(8,128)(2,1)S(1)}, bf16[1024,768]{1,0:T(8,128)(2,1)}, bf16[768,768]{1,0:T(8,128)(2,1)}) custom-call(s32[2]{0:T(128)S(1)} %pad_add_fusion.1.place, bf16[256,768]{1,0:T(8,128)(2,1)S(1)} %bitcast.69, bf16[192,768]{1,0:T(8,128)(2,1)S(1)} %get-tuple-element.229.refs_1_, bf16[352,768]{1,0:T(8,128)(2,1)} %collective-permute-done.26.refs_2_, ...), custom_call_target="tpu_custom_call" | custom-call | flops 1207959552 | bytes 6291456 | tf_op jit(solution)/shard_map/pallas_call | solution.py:424
  58.4 7.7 %shard_map.521 = (bf16[1024,256]{1,0:T(8,128)(2,1)S(1)}, f32[2,1024,2]{2,1,0:T(8,128)}) custom-call(s32[1024,1]{1,0:T(8,128)S(1)} %copy.69.refs_0_, s32[1,1024]{1,0:T(1,128)S(1)} %bitcast.78, bf16[1024,768]{1,0:T(8,128)(2,1)S(1)} %get-tuple-element.233.refs_2_.refs_3_.refs_4_, bf16[1024,768]{1,0:T(8,128)(2,1)S(1)} %get-tuple-element.233.refs_2_.refs_3_.refs_4_, ...), custom_call_target="tpu_custom_call" | custom-call | flops 4294967296 | bytes 2097152 | tf_op jit(solution)/shard_map/pallas_call | solution.py:249
  69.4 5.6 %collective-permute-done.32.refs_3_ = bf16[256,192]{1,0:T(8,128)(2,1)S(1)} collective-permute-done((bf16[256,192]{1,0:T(8,128)(2,1)S(1)}, bf16[256,192]{1,0:T(8,128)(2,1)S(1)}, u32[]{:S(2)}, u32[]{:S(2)}) %collective-permute-start.32) | collective-permute-done | bytes 98336 | tf_op jit(solution)/shard_map/ppermute | solution.py:31
  75.0 2.2 collective-permute-done.31.refs_2_
  77.2 3.5 collective-permute-done.30.refs_1_
  80.7 10.6 %all-gather.2.cloned.1.call-done.refs_5_.refs_6_.refs_7_.refs_12_.refs_13_.refs_14_ = bf16[9,768,768]{2,1,0:T(8,128)(2,1)} async-done(((bf16[9,24,768]{2,1,0:T(8,128)(2,1)}), bf16[9,768,768]{2,1,0:T(8,128)(2,1)}) %all-gather.2.cloned.1.call-update) | async-done | bytes 10616848 | tf_op jit(solution)/shard_map/all_gather | solution.py:932
  91.3 4.0 copy-done
  95.3 7.6 %shard_map.522 = (bf16[256,768]{1,0:T(8,128)(2,1)S(1)}, f32[256,768]{1,0:T(8,128)S(1)}, bf16[256,768]{1,0:T(8,128)(2,1)S(1)}, bf16[256,3072]{1,0:T(8,128)(2,1)S(...) custom-call(s32[2]{0:T(128)S(1)} %pad_add_fusion.1.place, ...), custom_call_target="tpu_custom_call" | custom-call | flops 3019898880 | bytes 11796480 | tf_op jit(solution)/shard_map/pallas_call | solution.py:493
  115.7 5.2 %shard_map.523 = (f32[1568,384]{1,0:T(8,128)S(1)}, bf16[1568,384]{1,0:T(8,128)(2,1)S(1)}, bf16[1568,1152]{1,0:T(8,128)(2,1)S(1)}) custom-call(bf16[64,384]{1,0:T(8,128)(2,1)S(1)} %get-tuple-element.235.refs_0_, bf16[64,384]{1,0:T(8,128)(2,1)S(1)} %collective-permute-done.33.refs_1_, bf16[64,384]{1,0:T(8,128)(2,1)S(1)} %collective-permute-done.34.refs_2_, ...), custom_call_target="tpu_custom_call" | custom-call | flops 1849688064 | bytes 9633792 | tf_op jit(solution)/shard_map/pallas_call | solution.py:686
  120.9 21.4 %shard_map.524 = (bf16[1568,384]{1,0:T(8,128)(2,1)S(1)}, f32[3,1568,2]{2,1,0:T(8,128)S(1)}) custom-call(bf16[1568,1152]{1,0:T(8,128)(2,1)S(1)} %get-tuple-element.240.refs_0_.refs_1_.refs_2_, bf16[1568,1152]{1,0:T(8,128)(2,1)S(1)} %get-tuple-element.240.refs_0_.refs_1_.refs_2_, bf16[1568,1152]{1,0:T(8,128)(2,1)S(1)} %get-tuple-element.240.refs_0_.refs_1_.refs_2_), custom_call_target="tpu_custom_call" | custom-call | flops 15105785856 | bytes 4816896 | tf_op jit(solution)/shard_map/pallas_call | solution.py:249
  143.8 22.2 %shard_map.525 = (bf16[1568,384]{1,0:T(8,128)(2,1)}, f32[1568,384]{1,0:T(8,128)S(1)}, bf16[1568,384]{1,0:T(8,128)(2,1)S(1)}, bf16[1568,384]{1,0:T(8,128)(2,1)S(1...) custom-call(f32[1568,384]{1,0:T(8,128)S(1)} %get-tuple-element.239.x, ...), custom_call_target="tpu_custom_call" | custom-call | flops 25895632896 | bytes 12042240 | tf_op jit(solution)/shard_map/pallas_call | solution.py:826
  167.7 38.3 %shard_map.526.grad = bf16[1568,1152]{1,0:T(8,128)(2,1)S(1)} custom-call(bf16[1568,1152]{1,0:T(8,128)(2,1)S(1)} %get-tuple-element.240.refs_0_.refs_1_.refs_2_, bf16[1568,1152]{1,0:T(8,128)(2,1)S(1)} %get-tuple-element.240.refs_0_.refs_1_.refs_2_, bf16[1568,1152]{1,0:T(8,128)(2,1)S(1)} %get-tuple-element.240.refs_0_.refs_1_.refs_2_, ...), custom_call_target="tpu_custom_call" | custom-call | flops 37764464640 | bytes 9633792 | tf_op jit(solution)/shard_map/pallas_call | solution.py:270
  206.0 5.5 %shard_map.527 = (bf16[64,384]{1,0:T(8,128)(2,1)S(1)}, bf16[64,384]{1,0:T(8,128)(2,1)S(1)}, bf16[64,384]{1,0:T(8,128)(2,1)S(1)}, bf16[64,384]{1,0:T(8,128)(2,1)S...) custom-call(bf16[1568,1152]{1,0:T(8,128)(2,1)S(1)} %shard_map.526.grad, ...), custom_call_target="tpu_custom_call" | custom-call | flops 1849688064 | bytes 9633792 | tf_op jit(solution)/shard_map/pallas_call | solution.py:729
  211.5 2.0 convolution_convert_fusion.2.refs_16_
  213.5 2.5 collective-permute-start.36
  217.6 2.9 collective-permute-done.37.refs_2_
  221.0 12.0 %shard_map.528 = (bf16[768,3072]{1,0:T(8,128)(2,1)}, bf16[3072,768]{1,0:T(8,128)(2,1)}, f32[1,3072]{1,0:T(1,128)}, f32[256,768]{1,0:T(8,128)}, bf16[768,768]{1,0...) custom-call(s32[2]{0:T(128)S(1)} %pad_add_fusion.1.place, ...), custom_call_target="tpu_custom_call" | custom-call | flops 6039797760 | bytes 23592960 | tf_op jit(solution)/shard_map/pallas_call | solution.py:570
  240.3 133.9 %conditional.1 = (f32[768,2304]{1,0:T(8,128)}, f32[768,256]{1,0:T(8,128)}, f32[1,256,768]{2,1,0:T(8,128)}) conditional(s32[]{:T(128)} %bitcast.27, () %tuple.21, (s32[]{:T(128)}, bf16[1024,768]{1,0:T(8,128)(2,1)}, bf16[1024,192]{1,0:T(8,128)(2,1)S(1)}, s32[1024,1]{0,1:T(1,128)S(1)}, s32[1,1024]{1,0:T(1,128)S(1)}, ...), branch_computations={%region_2.4_spmd, %region_3.5_spmd} | conditional | flops 13159375872 | bytes 66559516 | solution.py:1100
  241.5 12.1 %branch_1_fun.4.refs_4_ = bf16[1024,768]{1,0:T(8,128)(2,1)S(1)} custom-call(s32[1024,1]{1,0:T(8,128)S(1)} %copy.73.refs_0_, s32[1,1024]{1,0:T(1,128)S(1)} %get-tuple-element.83.refs_1_, bf16[1024,768]{1,0:T(8,128)(2,1)} %get-tuple-element.84.refs_2_.refs_3_.refs_4_, bf16[1024,768]{1,0:T(8,128)(2,1)} %get-tuple-element.84.refs_2_.refs_3_.refs_4_, ...), custom_call_target="tpu_custom_call" | custom-call | flops 10737418240 | bytes 4194304 | tf_op jit(solution)/shard_map/cond/branch_1_fun/pallas_call | solution.py:270
  253.7 4.2 branch_1_fun.5
  259.2 2.5 collective-permute-start.2
  262.3 2.0 convolution_convert_fusion
  264.4 2.0 collective-permute-done.1
  268.4 6.3 %collective-permute-start.3 = (bf16[384,640]{1,0:T(8,128)(2,1)S(1)}, bf16[384,640]{1,0:T(8,128)(2,1)S(1)}, u32[]{:S(2)}, u32[]{:S(2)}) collective-permute-start(bf16[384,640]{1,0:T(8,128)(2,1)S(1)} %pad_maximum_fusion), channel_id=1, source_target_pairs={{0,4},{4,0},{1,5},{5,1},{2,6},{6,2},{3,7},{7,3},{8,12},{12,8},{9,1... | collective-permute-start | bytes 1474568 | tf_op jit(solution)/shard_map/cond/branch_1_fun/ppermute | solution.py:35
  274.7 2.0 convolution_convert_fusion.1
  277.1 2.9 collective-permute-start.4
  281.6 2.0 collective-permute-done.4
  283.6 2.6 collective-permute-done.6
  286.6 3.0 collective-permute-start.7
  291.0 2.1 collective-permute-done.9
  296.5 1.9 collective-permute-done.12
  300.2 3.0 collective-permute-start.15
  303.9 5.7 %collective-permute-done.13 = bf16[96,640]{1,0:T(8,128)(2,1)S(1)} collective-permute-done((bf16[96,640]{1,0:T(8,128)(2,1)S(1)}, bf16[96,640]{1,0:T(8,128)(2,1)S(1)}, u32[]{:S(2)}, u32[]{:S(2)}) %collective-permute-start.13) | collective-permute-done | bytes 122912 | tf_op jit(solution)/shard_map/cond/branch_1_fun/ppermute | solution.py:31
  312.1 1.9 collective-permute-start.23
  315.2 23.5 %collective-permute-done.23.a = bf16[256,768]{1,0:T(8,128)(2,1)S(1)} collective-permute-done((bf16[256,768]{1,0:T(8,128)(2,1)S(1)}, bf16[256,768]{1,0:T(8,128)(2,1)S(1)}, u32[]{:S(2)}, u32[]{:S(2)}) %collective-permute-start.23) | collective-permute-done | bytes 393248 | tf_op jit(solution)/shard_map/cond/branch_1_fun/ppermute | solution.py:31
  339.5 10.3 %collective-permute-start.19 = (bf16[384,640]{1,0:T(8,128)(2,1)S(1)}, bf16[384,640]{1,0:T(8,128)(2,1)S(1)}, u32[]{:S(2)}, u32[]{:S(2)}) collective-permute-start(bf16[384,640]{1,0:T(8,128)(2,1)S(1)} %constant_dynamic-update-slice_fusion.19.refs_0_), channel_id=1, source_target_pairs={{0,4},{4,0},{1,5},{5,1},{2,6},{6,2},{3,7},{7,3},{8,12},{12,8},{9,1... | collective-permute-start | bytes 1474568 | tf_op jit(solution)/shard_map/cond/branch_1_fun/ppermute | solution.py:35
  351.2 9.5 %collective-permute-done.25.c = bf16[256,768]{1,0:T(8,128)(2,1)} collective-permute-done((bf16[256,768]{1,0:T(8,128)(2,1)}, bf16[256,768]{1,0:T(8,128)(2,1)}, u32[]{:S(2)}, u32[]{:S(2)}) %collective-permute-start.25) | collective-permute-done | bytes 393248 | tf_op jit(solution)/shard_map/cond/branch_1_fun/ppermute | solution.py:31
  362.6 3.0 branch_1_fun.7
  365.6 8.4 %branch_1_fun.6 = (f32[768,2304]{1,0:T(8,128)}, f32[768,256]{1,0:T(8,128)}) custom-call(s32[4]{0:T(128)S(1)} %pad_add_fusion.place, bf16[384,640]{1,0:T(8,128)(2,1)S(1)} %constant_dynamic-update-slice_fusion.19.refs_0_, bf16[384,640]{1,0:T(8,128)(2,1)S(1)} %collective-permute-done.16.refs_1_, bf16[384,640]{1,0:T(8,128)(2,1)S(1)} %collective-permute-done.17.refs_2_, ...), custom_call_target="tpu_custom_call" | custom-call | tf_op jit(solution)/shard_map/cond/branch_1_fun/pallas_call | solution.py:103
  377.7 43.1 %all-reduce.5.cloned.1.call-done = (bf16[384,1152]{1,0:T(8,128)(2,1)}, bf16[384,384]{1,0:T(8,128)(2,1)}, bf16[384,1536]{1,0:T(8,128)(2,1)}, bf16[1536,384]{1,0:T...) async-done(((bf16[384,1152]{1,0:T(8,128)(2,1)}, bf16[384,384]{1,0:T(8,128)(2,1)}, ...) | async-done | bytes 14745616 | tf_op jit(solution)/shard_map/psum | solution.py:1099
  420.8 2.3 copy-done.1
  423.1 2.3 copy-done.2
  432.5 9.8 %shard_map.529 = (f32[384,1152]{1,0:T(8,128)}, f32[384,384]{1,0:T(8,128)}, f32[384,1536]{1,0:T(8,128)}, f32[1536,384]{1,0:T(8,128)}, f32[768,768]{1,0:T(8,128)},...) custom-call(bf16[384,1152]{1,0:T(8,128)(2,1)S(1)} %copy-done.9, bf16[384,384]{1,0:T(8,128)(2,1)S(1)} %copy-done.26, ...), custom_call_target="tpu_custom_call" | custom-call | bytes 44236800 | tf_op jit(solution)/shard_map/pallas_call | solution.py:847
  (349 shorter events, 78.4 us)
Async XLA Ops:
  7.4 83.9 %all-gather.2.cloned.1.call-start = ((), (), s32[]{:S(2)}) async-start(), calls=%async_computation | async-start | bytes 10948608 | tf_op jit(solution)/shard_map/all_gather | solution.py:932
  13.2 407.6 %all-reduce.5.cloned.1.call-start = ((), (), s32[]{:S(2)}) async-start(), calls=%async_computation.1 | async-start | bytes 29491200 | tf_op jit(solution)/shard_map/psum | solution.py:1099
  15.4 15.0 %collective-permute-start.26 = (bf16[352,768]{1,0:T(8,128)(2,1)S(1)}, bf16[352,768]{1,0:T(8,128)(2,1)}, u32[]{:S(2)}, u32[]{:S(2)}) collective-permute-start(bf16[352,768]{1,0:T(8,128)(2,1)S(1)} %get-tuple-element.230), channel_id=1, source_target_pairs={{0,1},{1,2},{2,3},{3,0},{4,5},{5,6},{6,7},{7,4},{8,9},{9,10},{10,1... | collective-permute-start | bytes 1622024 | tf_op jit(solution)/shard_map/ppermute | solution.py:31
  17.5 36.2 %copy-start.35 = (bf16[1,256,768]{2,1,0:T(8,128)(2,1)S(1)}, bf16[1,256,768]{2,1,0:T(8,128)(2,1)}, u32[]{:S(2)}) copy-start(bf16[1,256,768]{2,1,0:T(8,128)(2,1)} %param.36) | copy-start | bytes 1179652
  17.5 31.2 %collective-permute-start.27 = (bf16[352,768]{1,0:T(8,128)(2,1)S(1)}, bf16[352,768]{1,0:T(8,128)(2,1)}, u32[]{:S(2)}, u32[]{:S(2)}) collective-permute-start(bf16[352,768]{1,0:T(8,128)(2,1)S(1)} %get-tuple-element.231), channel_id=1, source_target_pairs={{0,2},{1,3},{2,0},{3,1},{4,6},{5,7},{6,4},{7,5},{8,10},{9,11},{10,... | collective-permute-start | bytes 1622024 | tf_op jit(solution)/shard_map/ppermute | solution.py:31
  20.0 29.6 %collective-permute-start.28 = (bf16[352,768]{1,0:T(8,128)(2,1)S(1)}, bf16[352,768]{1,0:T(8,128)(2,1)}, u32[]{:S(2)}, u32[]{:S(2)}) collective-permute-start(bf16[352,768]{1,0:T(8,128)(2,1)S(1)} %get-tuple-element.232), channel_id=1, source_target_pairs={{0,3},{1,0},{2,1},{3,2},{4,7},{5,4},{6,5},{7,6},{8,11},{9,8},{10,9... | collective-permute-start | bytes 1622024 | tf_op jit(solution)/shard_map/ppermute | solution.py:31
  24.7 66.6 %copy-start.39 = (f32[1,14208]{1,0:T(1,128)}, f32[1,14208]{1,0:T(1,128)S(1)}, u32[]{:S(2)}) copy-start(f32[1,14208]{1,0:T(1,128)S(1)} %convert_element_type.92.refs_6_.refs_10_.refs_8_.vec.refs_15_) | copy-start | bytes 170500
  50.6 3.1 collective-permute-start.29
  66.9 8.1 %collective-permute-start.32 = (bf16[256,192]{1,0:T(8,128)(2,1)S(1)}, bf16[256,192]{1,0:T(8,128)(2,1)S(1)}, u32[]{:S(2)}, u32[]{:S(2)}) collective-permute-start(bf16[256,192]{1,0:T(8,128)(2,1)S(1)} %get-tuple-element.405), channel_id=1, source_target_pairs={{0,3},{1,0},{2,1},{3,2},{4,7},{5,4},{6,5},{7,6},{8,11},{9,8},{10,9... | collective-permute-start | bytes 294920 | tf_op jit(solution)/shard_map/ppermute | solution.py:31
  67.8 9.4 %collective-permute-start.31 = (bf16[256,192]{1,0:T(8,128)(2,1)S(1)}, bf16[256,192]{1,0:T(8,128)(2,1)S(1)}, u32[]{:S(2)}, u32[]{:S(2)}) collective-permute-start(bf16[256,192]{1,0:T(8,128)(2,1)S(1)} %get-tuple-element.406), channel_id=1, source_target_pairs={{0,2},{1,3},{2,0},{3,1},{4,6},{5,7},{6,4},{7,5},{8,10},{9,11},{10,... | collective-permute-start | bytes 294920 | tf_op jit(solution)/shard_map/ppermute | solution.py:31
  68.6 12.1 %collective-permute-start.30 = (bf16[256,192]{1,0:T(8,128)(2,1)S(1)}, bf16[256,192]{1,0:T(8,128)(2,1)S(1)}, u32[]{:S(2)}, u32[]{:S(2)}) collective-permute-start(bf16[256,192]{1,0:T(8,128)(2,1)S(1)} %get-tuple-element.407), channel_id=1, source_target_pairs={{0,1},{1,2},{2,3},{3,0},{4,5},{5,6},{6,7},{7,4},{8,9},{9,10},{10,1... | collective-permute-start | bytes 294920 | tf_op jit(solution)/shard_map/ppermute | solution.py:31
  107.2 5.5 %collective-permute-start.33 = (bf16[64,384]{1,0:T(8,128)(2,1)S(1)}, bf16[64,384]{1,0:T(8,128)(2,1)S(1)}, u32[]{:S(2)}, u32[]{:S(2)}) collective-permute-start(bf16[64,384]{1,0:T(8,128)(2,1)S(1)} %get-tuple-element.236), channel_id=1, source_target_pairs={{0,1},{1,2},{2,3},{3,0},{4,5},{5,6},{6,7},{7,4},{8,9},{9,10},{10,1... | collective-permute-start | bytes 147464 | tf_op jit(solution)/shard_map/ppermute | solution.py:31
  107.2 5.5 %collective-permute-start.34 = (bf16[64,384]{1,0:T(8,128)(2,1)S(1)}, bf16[64,384]{1,0:T(8,128)(2,1)S(1)}, u32[]{:S(2)}, u32[]{:S(2)}) collective-permute-start(bf16[64,384]{1,0:T(8,128)(2,1)S(1)} %get-tuple-element.237), channel_id=1, source_target_pairs={{0,2},{1,3},{2,0},{3,1},{4,6},{5,7},{6,4},{7,5},{8,10},{9,11},{10,... | collective-permute-start | bytes 147464 | tf_op jit(solution)/shard_map/ppermute | solution.py:31
  109.0 3.8 collective-permute-start.35
  167.7 38.3 %copy-start.12 = (bf16[384,1152]{1,0:T(8,128)(2,1)S(1)}, bf16[384,1152]{1,0:T(8,128)(2,1)}, u32[]{:S(2)}) copy-start(bf16[384,1152]{1,0:T(8,128)(2,1)} %weight.3) | copy-start | bytes 2654212
  213.5 4.1 collective-permute-start.36
  215.9 4.5 collective-permute-start.37
  216.6 4.3 collective-permute-start.38
  233.1 6.5 %collective-permute-start.39 = (bf16[256,192]{1,0:T(8,128)(2,1)S(1)}, bf16[256,192]{1,0:T(8,128)(2,1)S(1)}, u32[]{:S(2)}, u32[]{:S(2)}) collective-permute-start(bf16[256,192]{1,0:T(8,128)(2,1)S(1)} %get-tuple-element.266), channel_id=1, source_target_pairs={{0,1},{1,2},{2,3},{3,0},{4,5},{5,6},{6,7},{7,4},{8,9},{9,10},{10,1... | collective-permute-start | bytes 294920 | tf_op jit(solution)/shard_map/ppermute | solution.py:31
  233.2 6.4 %collective-permute-start.40 = (bf16[256,192]{1,0:T(8,128)(2,1)S(1)}, bf16[256,192]{1,0:T(8,128)(2,1)S(1)}, u32[]{:S(2)}, u32[]{:S(2)}) collective-permute-start(bf16[256,192]{1,0:T(8,128)(2,1)S(1)} %get-tuple-element.267), channel_id=1, source_target_pairs={{0,2},{1,3},{2,0},{3,1},{4,6},{5,7},{6,4},{7,5},{8,10},{9,11},{10,... | collective-permute-start | bytes 294920 | tf_op jit(solution)/shard_map/ppermute | solution.py:31
  234.6 5.5 %collective-permute-start.41 = (bf16[256,192]{1,0:T(8,128)(2,1)S(1)}, bf16[256,192]{1,0:T(8,128)(2,1)S(1)}, u32[]{:S(2)}, u32[]{:S(2)}) collective-permute-start(bf16[256,192]{1,0:T(8,128)(2,1)S(1)} %get-tuple-element.268), channel_id=1, source_target_pairs={{0,3},{1,0},{2,1},{3,2},{4,7},{5,4},{6,5},{7,6},{8,11},{9,8},{10,9... | collective-permute-start | bytes 294920 | tf_op jit(solution)/shard_map/ppermute | solution.py:31
  259.2 5.2 %collective-permute-start.2 = (f32[112,128]{1,0:T(8,128)S(1)}, f32[112,128]{1,0:T(8,128)S(1)}, u32[]{:S(2)}, u32[]{:S(2)}) collective-permute-start(f32[112,128]{1,0:T(8,128)S(1)} %bitcast.73), channel_id=1, source_target_pairs={{0,3},{1,0},{2,1},{3,2},{4,7},{5,4},{6,5},{7,6},{8,11},{9,8},{10,9... | collective-permute-start | bytes 172040 | tf_op jit(solution)/shard_map/cond/branch_1_fun/ppermute | solution.py:31
  261.7 4.7 %collective-permute-start.1 = (f32[112,128]{1,0:T(8,128)S(1)}, f32[112,128]{1,0:T(8,128)S(1)}, u32[]{:S(2)}, u32[]{:S(2)}) collective-permute-start(f32[112,128]{1,0:T(8,128)S(1)} %bitcast.74), channel_id=1, source_target_pairs={{0,2},{1,3},{2,0},{3,1},{4,6},{5,7},{6,4},{7,5},{8,10},{9,11},{10,... | collective-permute-start | bytes 172040 | tf_op jit(solution)/shard_map/cond/branch_1_fun/ppermute | solution.py:31
  261.7 5.5 %collective-permute-start = (f32[112,128]{1,0:T(8,128)S(1)}, f32[112,128]{1,0:T(8,128)}, u32[]{:S(2)}, u32[]{:S(2)}) collective-permute-start(f32[112,128]{1,0:T(8,128)S(1)} %bitcast.75), channel_id=1, source_target_pairs={{0,1},{1,2},{2,3},{3,0},{4,5},{5,6},{6,7},{7,4},{8,9},{9,10},{10,1... | collective-permute-start | bytes 172040 | tf_op jit(solution)/shard_map/cond/branch_1_fun/ppermute | solution.py:31
  268.4 8.3 %collective-permute-start.3 = (bf16[384,640]{1,0:T(8,128)(2,1)S(1)}, bf16[384,640]{1,0:T(8,128)(2,1)S(1)}, u32[]{:S(2)}, u32[]{:S(2)}) collective-permute-start(bf16[384,640]{1,0:T(8,128)(2,1)S(1)} %pad_maximum_fusion), channel_id=1, source_target_pairs={{0,4},{4,0},{1,5},{5,1},{2,6},{6,2},{3,7},{7,3},{8,12},{12,8},{9,1... | collective-permute-start | bytes 1474568 | tf_op jit(solution)/shard_map/cond/branch_1_fun/ppermute | solution.py:35
  277.0 83.6 %copy-start.43 = (f32[1,14208]{1,0:T(1,128)S(1)}, f32[1,14208]{1,0:T(1,128)}, u32[]{:S(2)}) copy-start(f32[1,14208]{1,0:T(1,128)} %copy-done.42) | copy-start | bytes 170500 | tf_op jit(solution)/shard_map/cond
  277.1 6.5 %collective-permute-start.4 = (bf16[96,640]{1,0:T(8,128)(2,1)S(1)}, bf16[96,640]{1,0:T(8,128)(2,1)S(1)}, u32[]{:S(2)}, u32[]{:S(2)}) collective-permute-start(bf16[96,640]{1,0:T(8,128)(2,1)S(1)} %get-tuple-element.389), channel_id=1, source_target_pairs={{0,16},{8,24},{16,0},{24,8},{1,17},{9,25},{17,1},{25,9},{2,18},{10... | collective-permute-start | bytes 368648 | tf_op jit(solution)/shard_map/cond/branch_1_fun/ppermute | solution.py:31
  279.9 6.3 %collective-permute-start.6 = (bf16[96,640]{1,0:T(8,128)(2,1)S(1)}, bf16[96,640]{1,0:T(8,128)(2,1)S(1)}, u32[]{:S(2)}, u32[]{:S(2)}) collective-permute-start(bf16[96,640]{1,0:T(8,128)(2,1)S(1)} %get-tuple-element.390), channel_id=1, source_target_pairs={{0,24},{8,0},{16,8},{24,16},{1,25},{9,1},{17,9},{25,17},{2,26},{10... | collective-permute-start | bytes 368648 | tf_op jit(solution)/shard_map/cond/branch_1_fun/ppermute | solution.py:31
  280.7 5.7 %collective-permute-start.5 = (bf16[96,640]{1,0:T(8,128)(2,1)S(1)}, bf16[96,640]{1,0:T(8,128)(2,1)S(1)}, u32[]{:S(2)}, u32[]{:S(2)}) collective-permute-start(bf16[96,640]{1,0:T(8,128)(2,1)S(1)} %get-tuple-element.391), channel_id=1, source_target_pairs={{0,8},{8,16},{16,24},{24,0},{1,9},{9,17},{17,25},{25,1},{2,10},{10... | collective-permute-start | bytes 368648 | tf_op jit(solution)/shard_map/cond/branch_1_fun/ppermute | solution.py:31
  286.6 4.5 collective-permute-start.7
  289.6 3.5 collective-permute-start.9
  290.3 4.6 %collective-permute-start.8 = (bf16[24,640]{1,0:T(8,128)(2,1)S(1)}, bf16[24,640]{1,0:T(8,128)(2,1)S(1)}, u32[]{:S(2)}, u32[]{:S(2)}) collective-permute-start(bf16[24,640]{1,0:T(8,128)(2,1)S(1)} %get-tuple-element.400), channel_id=1, source_target_pairs={{0,32},{32,64},{64,96},{96,0},{1,33},{33,65},{65,97},{97,1},{2,34}... | collective-permute-start | bytes 92168 | tf_op jit(solution)/shard_map/cond/branch_1_fun/ppermute | solution.py:31
  295.0 3.4 collective-permute-start.12
  295.1 4.5 %collective-permute-start.11 = (bf16[24,640]{1,0:T(8,128)(2,1)S(1)}, bf16[24,640]{1,0:T(8,128)(2,1)S(1)}, u32[]{:S(2)}, u32[]{:S(2)}) collective-permute-start(bf16[24,640]{1,0:T(8,128)(2,1)S(1)} %get-tuple-element.388), channel_id=1, source_target_pairs={{0,64},{32,96},{64,0},{96,32},{1,65},{33,97},{65,1},{97,33},{2,66}... | collective-permute-start | bytes 92168 | tf_op jit(solution)/shard_map/cond/branch_1_fun/ppermute | solution.py:31
  296.0 4.1 collective-permute-start.10
  300.2 9.5 %collective-permute-start.15 = (bf16[96,640]{1,0:T(8,128)(2,1)S(1)}, bf16[96,640]{1,0:T(8,128)(2,1)S(1)}, u32[]{:S(2)}, u32[]{:S(2)}) collective-permute-start(bf16[96,640]{1,0:T(8,128)(2,1)S(1)} %pad_maximum_fusion.1), channel_id=1, source_target_pairs={{0,24},{8,0},{16,8},{24,16},{1,25},{9,1},{17,9},{25,17},{2,26},{10... | collective-permute-start | bytes 368648 | tf_op jit(solution)/shard_map/cond/branch_1_fun/ppermute | solution.py:31
  303.2 6.5 %collective-permute-start.14 = (bf16[96,640]{1,0:T(8,128)(2,1)S(1)}, bf16[96,640]{1,0:T(8,128)(2,1)S(1)}, u32[]{:S(2)}, u32[]{:S(2)}) collective-permute-start(bf16[96,640]{1,0:T(8,128)(2,1)S(1)} %pad_maximum_fusion.1), channel_id=1, source_target_pairs={{0,16},{8,24},{16,0},{24,8},{1,17},{9,25},{17,1},{25,9},{2,18},{10... | collective-permute-start | bytes 368648 | tf_op jit(solution)/shard_map/cond/branch_1_fun/ppermute | solution.py:31
  303.4 6.3 %collective-permute-start.13 = (bf16[96,640]{1,0:T(8,128)(2,1)S(1)}, bf16[96,640]{1,0:T(8,128)(2,1)S(1)}, u32[]{:S(2)}, u32[]{:S(2)}) collective-permute-start(bf16[96,640]{1,0:T(8,128)(2,1)S(1)} %pad_maximum_fusion.1), channel_id=1, source_target_pairs={{0,8},{8,16},{16,24},{24,0},{1,9},{9,17},{17,25},{25,1},{2,10},{10... | collective-permute-start | bytes 368648 | tf_op jit(solution)/shard_map/cond/branch_1_fun/ppermute | solution.py:31
  309.8 40.0 %collective-permute-start.18 = (bf16[384,640]{1,0:T(8,128)(2,1)S(1)}, bf16[384,640]{1,0:T(8,128)(2,1)S(1)}, u32[]{:S(2)}, u32[]{:S(2)}) collective-permute-start(bf16[384,640]{1,0:T(8,128)(2,1)S(1)} %constant_dynamic-update-slice_fusion.19.refs_0_), channel_id=1, source_target_pairs={{0,3},{1,0},{2,1},{3,2},{4,7},{5,4},{6,5},{7,6},{8,11},{9,8},{10,9... | collective-permute-start | bytes 1474568 | tf_op jit(solution)/shard_map/cond/branch_1_fun/ppermute | solution.py:31
  310.8 39.0 %collective-permute-start.17 = (bf16[384,640]{1,0:T(8,128)(2,1)S(1)}, bf16[384,640]{1,0:T(8,128)(2,1)S(1)}, u32[]{:S(2)}, u32[]{:S(2)}) collective-permute-start(bf16[384,640]{1,0:T(8,128)(2,1)S(1)} %constant_dynamic-update-slice_fusion.19.refs_0_), channel_id=1, source_target_pairs={{0,2},{1,3},{2,0},{3,1},{4,6},{5,7},{6,4},{7,5},{8,10},{9,11},{10,... | collective-permute-start | bytes 1474568 | tf_op jit(solution)/shard_map/cond/branch_1_fun/ppermute | solution.py:31
  311.3 39.0 %collective-permute-start.16 = (bf16[384,640]{1,0:T(8,128)(2,1)S(1)}, bf16[384,640]{1,0:T(8,128)(2,1)S(1)}, u32[]{:S(2)}, u32[]{:S(2)}) collective-permute-start(bf16[384,640]{1,0:T(8,128)(2,1)S(1)} %constant_dynamic-update-slice_fusion.19.refs_0_), channel_id=1, source_target_pairs={{0,1},{1,2},{2,3},{3,0},{4,5},{5,6},{6,7},{7,4},{8,9},{9,10},{10,1... | collective-permute-start | bytes 1474568 | tf_op jit(solution)/shard_map/cond/branch_1_fun/ppermute | solution.py:31
  312.1 26.7 %collective-permute-start.23 = (bf16[256,768]{1,0:T(8,128)(2,1)S(1)}, bf16[256,768]{1,0:T(8,128)(2,1)S(1)}, u32[]{:S(2)}, u32[]{:S(2)}) collective-permute-start(bf16[256,768]{1,0:T(8,128)(2,1)S(1)} %get-tuple-element.124), channel_id=1, source_target_pairs={{0,3},{1,0},{2,1},{3,2},{4,7},{5,4},{6,5},{7,6},{8,11},{9,8},{10,9... | collective-permute-start | bytes 1179656 | tf_op jit(solution)/shard_map/cond/branch_1_fun/ppermute | solution.py:31
  314.0 36.4 %collective-permute-start.24 = (bf16[256,768]{1,0:T(8,128)(2,1)}, bf16[256,768]{1,0:T(8,128)(2,1)S(1)}, u32[]{:S(2)}, u32[]{:S(2)}) collective-permute-start(bf16[256,768]{1,0:T(8,128)(2,1)} %get-tuple-element.125), channel_id=1, source_target_pairs={{0,2},{1,3},{2,0},{3,1},{4,6},{5,7},{6,4},{7,5},{8,10},{9,11},{10,... | collective-permute-start | bytes 1179656 | tf_op jit(solution)/shard_map/cond/branch_1_fun/ppermute | solution.py:31
  339.5 26.1 %collective-permute-start.19 = (bf16[384,640]{1,0:T(8,128)(2,1)S(1)}, bf16[384,640]{1,0:T(8,128)(2,1)S(1)}, u32[]{:S(2)}, u32[]{:S(2)}) collective-permute-start(bf16[384,640]{1,0:T(8,128)(2,1)S(1)} %constant_dynamic-update-slice_fusion.19.refs_0_), channel_id=1, source_target_pairs={{0,4},{4,0},{1,5},{5,1},{2,6},{6,2},{3,7},{7,3},{8,12},{12,8},{9,1... | collective-permute-start | bytes 1474568 | tf_op jit(solution)/shard_map/cond/branch_1_fun/ppermute | solution.py:35
  349.7 15.9 %collective-permute-start.22 = (bf16[384,640]{1,0:T(8,128)(2,1)S(1)}, bf16[384,640]{1,0:T(8,128)(2,1)}, u32[]{:S(2)}, u32[]{:S(2)}) collective-permute-start(bf16[384,640]{1,0:T(8,128)(2,1)S(1)} %collective-permute-done.18.refs_3_), channel_id=1, source_target_pairs={{0,4},{4,0},{1,5},{5,1},{2,6},{6,2},{3,7},{7,3},{8,12},{12,8},{9,1... | collective-permute-start | bytes 1474568 | tf_op jit(solution)/shard_map/cond/branch_1_fun/ppermute | solution.py:35
  349.7 15.8 %collective-permute-start.21 = (bf16[384,640]{1,0:T(8,128)(2,1)S(1)}, bf16[384,640]{1,0:T(8,128)(2,1)}, u32[]{:S(2)}, u32[]{:S(2)}) collective-permute-start(bf16[384,640]{1,0:T(8,128)(2,1)S(1)} %collective-permute-done.17.refs_2_), channel_id=1, source_target_pairs={{0,4},{4,0},{1,5},{5,1},{2,6},{6,2},{3,7},{7,3},{8,12},{12,8},{9,1... | collective-permute-start | bytes 1474568 | tf_op jit(solution)/shard_map/cond/branch_1_fun/ppermute | solution.py:35
  350.3 15.3 %collective-permute-start.20 = (bf16[384,640]{1,0:T(8,128)(2,1)S(1)}, bf16[384,640]{1,0:T(8,128)(2,1)}, u32[]{:S(2)}, u32[]{:S(2)}) collective-permute-start(bf16[384,640]{1,0:T(8,128)(2,1)S(1)} %collective-permute-done.16.refs_1_), channel_id=1, source_target_pairs={{0,4},{4,0},{1,5},{5,1},{2,6},{6,2},{3,7},{7,3},{8,12},{12,8},{9,1... | collective-permute-start | bytes 1474568 | tf_op jit(solution)/shard_map/cond/branch_1_fun/ppermute | solution.py:35
  351.1 9.5 %collective-permute-start.25 = (bf16[256,768]{1,0:T(8,128)(2,1)}, bf16[256,768]{1,0:T(8,128)(2,1)}, u32[]{:S(2)}, u32[]{:S(2)}) collective-permute-start(bf16[256,768]{1,0:T(8,128)(2,1)} %copy-done.30), channel_id=1, source_target_pairs={{0,1},{1,2},{2,3},{3,0},{4,5},{5,6},{6,7},{7,4},{8,9},{9,10},{10,1... | collective-permute-start | bytes 1179656 | tf_op jit(solution)/shard_map/cond/branch_1_fun/ppermute | solution.py:31
  (82 other events, 735.8 us)
Sparse Core Ops, SparseCore 0:
  13.3 77.9 all-gather.1
  233.2 187.5 all-reduce.4
where the time goes:
time: 458 us; the launch traced here: 450 us
  Pallas kernels  164 us (36%)
  waiting for transfers between devices  149 us (33%)
  starting transfers between devices  59.3 us (13%)
  local copies, waits for them, and re-layouts  49.4 us (11%)
  between operations  16.1 us (4%)
  matrix products  6.81 us (1%)
    ppermute x36, waiting for transfers between devices, shift(): return lax.ppermute(value, axis, [(i, (i + step) % 4) for i in range(4)])  94.2 us
    pallas_call x2, Pallas kernels, attend_back(): pl.pallas_call(functools.partial(backward_kernel, block=block, masked=mas...  50.4 us
    psum x1, waiting for transfers between devices, body(): rest_grads = lax.psum(early, ALL)  43.1 us
    ppermute x36, starting transfers between devices, shift(): return lax.ppermute(value, axis, [(i, (i + step) % 4) for i in range(4)])  40.4 us
    unnamed x149, local copies, waits for them, and re-layouts  32.5 us
    pallas_call x2, Pallas kernels, attend(): pl.pallas_call(functools.partial(forward_kernel, block=block, masked=mask...  29.1 us
    pallas_call x1, Pallas kernels, dec_mid(): pl.pallas_call(functools.partial(dec_mid_kernel, vectors=vectors, chunk=c...  22.2 us
    ppermute x6, starting transfers between devices, swap(): return lax.ppermute(value, 'core', [(0, 1), (1, 0)])  18.8 us
  transfers between devices with their start and end apart: 44, of which 27 were waited for; matrix products, arithmetic and copies ran while one was open for 5% of the time, Pallas kernels for 9%

commit v1 on v0

--- a/solution.py
+++ b/solution.py
@@ -345,7 +345,19 @@
         return ref[:, at : at + (self.size[name] - first if count is None else count)]
 
 
-def group_kernel(place, weight, inputs, *outs):
+def start_kernel(place, weight, inputs, fc2, proj, fc1, *outs):
+    strip = outs[4]
+    eighth = strip.shape[1]
+    for v in range(8):
+
+        @pl.when(place[2] == v)
+        def _():
+            rows = slice(v * eighth, (v + 1) * eighth)
+            for b in range(4):
+                strip[b] = fc2[b * 192 + rows.start : b * 192 + rows.stop, :]
+                strip[5 + b] = fc1[rows, b * 768 : (b + 1) * 768]
+            strip[4] = proj[rows, :]
+
     width = weight.shape[1] // 3
     part = width // 4
     rows = inputs.shape[0]
@@ -371,21 +383,22 @@
                 outs[k][rows:, :] = own
 
 
-def group_pieces(weight, inputs, place):
+def start(weight, inputs, fc2, proj, fc1, place):
     rows, count = weight.shape[0], inputs.shape[0]
     outs = [shape(rows, 768, BF16)] + [shape(count + rows // 2, 768, BF16)] * 3
-    whole = lambda a: pl.BlockSpec(a.shape, lambda i, s: (0, 0))
-    return pl.pallas_call(
-        group_kernel,
+    outs.append(jax.ShapeDtypeStruct((9, rows // 8, 768), BF16))
+    whole = lambda a: pl.BlockSpec(a.shape, lambda i, s: (0,) * len(a.shape))
+    return pl.pallas_call(
+        start_kernel,
         grid_spec=pltpu.PrefetchScalarGridSpec(
             num_scalar_prefetch=1,
             grid=(1,),
-            in_specs=[whole(weight), whole(inputs)],
+            in_specs=[whole(a) for a in (weight, inputs, fc2, proj, fc1)],
             out_specs=[whole(a) for a in outs],
         ),
         out_shape=outs,
-        compiler_params=room(10),
-    )(place, weight, inputs)
+        compiler_params=room(24),
+    )(place, weight, inputs, fc2, proj, fc1)
 
 
 def enc_in_kernel(place, *refs, vectors):
@@ -850,7 +863,7 @@
         in_specs=[piece(a) for a in arrays],
         out_specs=[piece(a) for a in arrays],
         out_shape=[shape(*a.shape, F32) for a in arrays],
-        compiler_params=room(16),
+        compiler_params=room(56),
         cost_estimate=cost(0, sum(a.shape[0] * a.shape[1] * 6 for a in arrays)),
     )(*arrays)
 
@@ -890,7 +903,7 @@
 ):
     x_at = lax.axis_index("x")
     core = lax.axis_index("core")
-    place = place_of(("x", "core"))
+    place = jnp.stack([x_at, core, core * 4 + lax.axis_index("y")]).astype(jnp.int32)
     tokens, width = encoder_input.shape[1:]
     hw = width // 4
     vectors = Vectors(
@@ -916,22 +929,14 @@
     )
 
     own_input = encoder_input[0]
-    piece, *others = exchange(group_pieces(enc_qkv_weight, own_input, place), "x")
+    *pieces, strip = start(
+        enc_qkv_weight, own_input, enc_fc2_weight, enc_proj_weight, enc_fc1_weight, place
+    )
+    piece, *others = exchange(pieces, "x")
     swapped = swap(jnp.concatenate([other[tokens:] for other in others], axis=0))
     inputs = [own_input, *others]
 
-    eighth = hw // 8
-    first_row = (core * 4 + lax.axis_index("y")) * eighth
-    rows_of = lambda stack: lax.dynamic_slice_in_dim(stack, first_row, eighth, 1)
-    strip = [
-        rows_of(enc_fc2_weight.reshape(4, hw, width)),
-        rows_of(enc_proj_weight[None]),
-    ]
-    fc1_rows = lax.dynamic_slice_in_dim(enc_fc1_weight, first_row, eighth, 0)
-    strip += [fc1_rows[None, :, k * width : (k + 1) * width] for k in range(4)]
-    matrices = lax.all_gather(
-        jnp.concatenate(strip, axis=0), ("x", "core", "y"), axis=1, tiled=True
-    )
+    matrices = lax.all_gather(strip, ("x", "core", "y"), axis=1, tiled=True)
 
     row_seg = seg_ids[0].reshape(4, tokens)
     row_slot = vis_slot[0].reshape(4, tokens)

time: 458 us -> 448 us (0.978)
  local copies, waits for them, and re-layouts: 49.4 us -> 34.2 us
  Pallas kernels: 164 us -> 171 us
    unnamed x149 -> x140, local copies, waits for them, and re-layouts: 32.5 us -> 19.8 us
    pallas_call x1, Pallas kernels: 9.79 us -> 16.4 us  [widen(): pl.pallas_call(widen_kernel, grid=(8,), in_specs=[piece(a) for a in array...]
  transfers between devices with their start and end apart: 44 -> 44, of which waited for: 27 -> 28; matrix products, arithmetic and copies ran while one was open for 5% -> 5% of each run, Pallas kernels for 9% -> 9%
where the time goes in v1:
time: 448 us; the launch traced here: 440 us
  Pallas kernels  171 us (38%)
  waiting for transfers between devices  149 us (33%)
  starting transfers between devices  57.5 us (13%)
  local copies, waits for them, and re-layouts  34.2 us (8%)
  between operations  16.1 us (4%)
  matrix products  6.77 us (2%)
  other arithmetic  4.63 us (1%)
    ppermute x36, waiting for transfers between devices, shift(): return lax.ppermute(value, axis, [(i, (i + step) % 4) for i in range(4)])  96.8 us
    pallas_call x2, Pallas kernels, attend_back(): pl.pallas_call(functools.partial(backward_kernel, block=block, masked=mas...  50.5 us
    psum x1, waiting for transfers between devices, body(): rest_grads = lax.psum(early, ALL)  40 us
    ppermute x36, starting transfers between devices, shift(): return lax.ppermute(value, axis, [(i, (i + step) % 4) for i in range(4)])  39.8 us
    pallas_call x2, Pallas kernels, attend(): pl.pallas_call(functools.partial(forward_kernel, block=block, masked=mask...  29.1 us
    pallas_call x1, Pallas kernels, dec_mid(): pl.pallas_call(functools.partial(dec_mid_kernel, vectors=vectors, chunk=c...  22.2 us
    unnamed x140, local copies, waits for them, and re-layouts  19.8 us
    ppermute x6, starting transfers between devices, swap(): return lax.ppermute(value, 'core', [(0, 1), (1, 0)])  17.6 us
  transfers between devices with their start and end apart: 44, of which 28 were waited for; matrix products, arithmetic and copies ran while one was open for 5% of the time, Pallas kernels for 9%

profile of v1, /device:TPU:1, one launch (start us, length us, event | category | flops | bytes accessed | tf_op | source)
XLA Modules:
  0.0 439.8 jit_solution(12960345947030697817)
XLA Ops:
  12.2 2.9 shard_map.519
  15.2 2.1 collective-permute-start.26
  17.3 2.5 collective-permute-start.27
  26.4 3.7 collective-permute-done.26.refs_2_
  30.1 18.3 %collective-permute-done.27.refs_3_ = bf16[352,768]{1,0:T(8,128)(2,1)} collective-permute-done((bf16[352,768]{1,0:T(8,128)(2,1)S(1)}, bf16[352,768]{1,0:T(8,128)(2,1)}, u32[]{:S(2)}, u32[]{:S(2)}) %collective-permute-start.27) | collective-permute-done | bytes 540704 | tf_op jit(solution)/shard_map/ppermute | solution.py:31
  53.4 4.5 %shard_map.520 = (bf16[1024,768]{1,0:T(8,128)(2,1)S(1)}, bf16[1024,768]{1,0:T(8,128)(2,1)}, bf16[768,768]{1,0:T(8,128)(2,1)}) custom-call(s32[3]{0:T(128)S(1)} %pad_add_fusion.1.place, bf16[256,768]{1,0:T(8,128)(2,1)S(1)} %bitcast.51, bf16[192,768]{1,0:T(8,128)(2,1)S(1)} %get-tuple-element.230.refs_1_, bf16[352,768]{1,0:T(8,128)(2,1)S(1)} %collective-permute-done.26.refs_2_, ...), custom_call_target="tpu_custom_call" | custom-call | flops 1207959552 | bytes 6291456 | tf_op jit(solution)/shard_map/pallas_call | solution.py:437
  58.0 7.7 %shard_map.521 = (bf16[1024,256]{1,0:T(8,128)(2,1)S(1)}, f32[2,1024,2]{2,1,0:T(8,128)}) custom-call(s32[1024,1]{1,0:T(8,128)S(1)} %copy.69.refs_0_, s32[1,1024]{1,0:T(1,128)S(1)} %bitcast.60, bf16[1024,768]{1,0:T(8,128)(2,1)S(1)} %get-tuple-element.234.refs_2_.refs_3_.refs_4_, bf16[1024,768]{1,0:T(8,128)(2,1)S(1)} %get-tuple-element.234.refs_2_.refs_3_.refs_4_, ...), custom_call_target="tpu_custom_call" | custom-call | flops 4294967296 | bytes 2097152 | tf_op jit(solution)/shard_map/pallas_call | solution.py:249
  68.4 5.6 %collective-permute-done.32.refs_3_ = bf16[256,192]{1,0:T(8,128)(2,1)S(1)} collective-permute-done((bf16[256,192]{1,0:T(8,128)(2,1)S(1)}, bf16[256,192]{1,0:T(8,128)(2,1)S(1)}, u32[]{:S(2)}, u32[]{:S(2)}) %collective-permute-start.32) | collective-permute-done | bytes 98336 | tf_op jit(solution)/shard_map/ppermute | solution.py:31
  74.0 2.2 collective-permute-done.31.refs_2_
  76.2 3.5 collective-permute-done.30.refs_1_
  79.7 10.8 %all-gather.2.cloned.1.call-done.refs_5_.refs_6_.refs_7_.refs_12_.refs_13_.refs_14_ = bf16[9,768,768]{2,1,0:T(8,128)(2,1)} async-done(((bf16[9,24,768]{2,1,0:T(8,128)(2,1)}), bf16[9,768,768]{2,1,0:T(8,128)(2,1)}) %all-gather.2.cloned.1.call-update) | async-done | bytes 10616848 | tf_op jit(solution)/shard_map/all_gather | solution.py:939
  90.5 4.0 copy-done
  94.5 7.6 %shard_map.522 = (bf16[256,768]{1,0:T(8,128)(2,1)S(1)}, f32[256,768]{1,0:T(8,128)S(1)}, bf16[256,768]{1,0:T(8,128)(2,1)S(1)}, bf16[256,3072]{1,0:T(8,128)(2,1)S(...) custom-call(s32[3]{0:T(128)S(1)} %pad_add_fusion.1.place, ...), custom_call_target="tpu_custom_call" | custom-call | flops 3019898880 | bytes 11796480 | tf_op jit(solution)/shard_map/pallas_call | solution.py:506
  106.4 1.7 collective-permute-start.34
  114.8 5.2 %shard_map.523 = (f32[1568,384]{1,0:T(8,128)S(1)}, bf16[1568,384]{1,0:T(8,128)(2,1)S(1)}, bf16[1568,1152]{1,0:T(8,128)(2,1)S(1)}) custom-call(bf16[64,384]{1,0:T(8,128)(2,1)S(1)} %get-tuple-element.237.refs_0_, bf16[64,384]{1,0:T(8,128)(2,1)S(1)} %collective-permute-done.33.refs_1_, bf16[64,384]{1,0:T(8,128)(2,1)S(1)} %collective-permute-done.34.refs_2_, ...), custom_call_target="tpu_custom_call" | custom-call | flops 1849688064 | bytes 9633792 | tf_op jit(solution)/shard_map/pallas_call | solution.py:699
  120.1 21.4 %shard_map.524 = (bf16[1568,384]{1,0:T(8,128)(2,1)S(1)}, f32[3,1568,2]{2,1,0:T(8,128)S(1)}) custom-call(bf16[1568,1152]{1,0:T(8,128)(2,1)S(1)} %get-tuple-element.242.refs_0_.refs_1_.refs_2_, bf16[1568,1152]{1,0:T(8,128)(2,1)S(1)} %get-tuple-element.242.refs_0_.refs_1_.refs_2_, bf16[1568,1152]{1,0:T(8,128)(2,1)S(1)} %get-tuple-element.242.refs_0_.refs_1_.refs_2_), custom_call_target="tpu_custom_call" | custom-call | flops 15105785856 | bytes 4816896 | tf_op jit(solution)/shard_map/pallas_call | solution.py:249
  143.0 22.2 %shard_map.525 = (bf16[1568,384]{1,0:T(8,128)(2,1)}, f32[1568,384]{1,0:T(8,128)S(1)}, bf16[1568,384]{1,0:T(8,128)(2,1)S(1)}, bf16[1568,384]{1,0:T(8,128)(2,1)S(1...) custom-call(f32[1568,384]{1,0:T(8,128)S(1)} %get-tuple-element.241.x, ...), custom_call_target="tpu_custom_call" | custom-call | flops 25895632896 | bytes 12042240 | tf_op jit(solution)/shard_map/pallas_call | solution.py:839
  166.8 38.3 %shard_map.526.grad = bf16[1568,1152]{1,0:T(8,128)(2,1)S(1)} custom-call(bf16[1568,1152]{1,0:T(8,128)(2,1)S(1)} %get-tuple-element.242.refs_0_.refs_1_.refs_2_, bf16[1568,1152]{1,0:T(8,128)(2,1)S(1)} %get-tuple-element.242.refs_0_.refs_1_.refs_2_, bf16[1568,1152]{1,0:T(8,128)(2,1)S(1)} %get-tuple-element.242.refs_0_.refs_1_.refs_2_, ...), custom_call_target="tpu_custom_call" | custom-call | flops 37764464640 | bytes 9633792 | tf_op jit(solution)/shard_map/pallas_call | solution.py:270
  205.2 5.5 %shard_map.527 = (bf16[64,384]{1,0:T(8,128)(2,1)S(1)}, bf16[64,384]{1,0:T(8,128)(2,1)S(1)}, bf16[64,384]{1,0:T(8,128)(2,1)S(1)}, bf16[64,384]{1,0:T(8,128)(2,1)S...) custom-call(bf16[1568,1152]{1,0:T(8,128)(2,1)S(1)} %shard_map.526.grad, ...), custom_call_target="tpu_custom_call" | custom-call | flops 1849688064 | bytes 9633792 | tf_op jit(solution)/shard_map/pallas_call | solution.py:742
  210.7 2.0 convolution_convert_fusion.2.refs_16_
  212.6 2.5 collective-permute-start.36
  216.7 2.9 collective-permute-done.37.refs_2_
  220.2 12.0 %shard_map.528 = (bf16[768,3072]{1,0:T(8,128)(2,1)}, bf16[3072,768]{1,0:T(8,128)(2,1)}, f32[1,3072]{1,0:T(1,128)S(1)}, f32[256,768]{1,0:T(8,128)}, bf16[768,768]...) custom-call(s32[3]{0:T(128)S(1)} %pad_add_fusion.1.place, ...), custom_call_target="tpu_custom_call" | custom-call | flops 6039797760 | bytes 23592960 | tf_op jit(solution)/shard_map/pallas_call | solution.py:583
  239.5 134.0 %conditional.1 = (f32[768,2304]{1,0:T(8,128)}, f32[768,256]{1,0:T(8,128)S(1)}, f32[1,256,768]{2,1,0:T(8,128)}) conditional(s32[]{:T(128)} %bitcast.22, () %tuple.21, (s32[]{:T(128)}, bf16[1024,768]{1,0:T(8,128)(2,1)}, bf16[1024,192]{1,0:T(8,128)(2,1)S(1)}, s32[1024,1]{0,1:T(1,128)S(1)}, s32[1,1024]{1,0:T(1,128)S(1)}, ...), branch_computations={%region_2.4_spmd, %region_3.5_spmd} | conditional | flops 13159375872 | bytes 67505696 | solution.py:1105
  239.9 12.2 %branch_1_fun.4.refs_4_ = bf16[1024,768]{1,0:T(8,128)(2,1)S(1)} custom-call(s32[1024,1]{1,0:T(8,128)S(1)} %copy.73.refs_0_, s32[1,1024]{1,0:T(1,128)S(1)} %get-tuple-element.83.refs_1_, bf16[1024,768]{1,0:T(8,128)(2,1)} %get-tuple-element.84.refs_2_.refs_3_.refs_4_, bf16[1024,768]{1,0:T(8,128)(2,1)} %get-tuple-element.84.refs_2_.refs_3_.refs_4_, ...), custom_call_target="tpu_custom_call" | custom-call | flops 10737418240 | bytes 4194304 | tf_op jit(solution)/shard_map/cond/branch_1_fun/pallas_call | solution.py:270
  252.3 3.9 branch_1_fun.5
  257.5 2.5 collective-permute-start.2
  260.6 2.0 convolution_convert_fusion
  262.7 2.3 collective-permute-done.1
  267.0 6.3 %collective-permute-start.3 = (bf16[384,640]{1,0:T(8,128)(2,1)S(1)}, bf16[384,640]{1,0:T(8,128)(2,1)S(1)}, u32[]{:S(2)}, u32[]{:S(2)}) collective-permute-start(bf16[384,640]{1,0:T(8,128)(2,1)S(1)} %pad_maximum_fusion), channel_id=1, source_target_pairs={{0,4},{4,0},{1,5},{5,1},{2,6},{6,2},{3,7},{7,3},{8,12},{12,8},{9,1... | collective-permute-start | bytes 1474568 | tf_op jit(solution)/shard_map/cond/branch_1_fun/ppermute | solution.py:35
  273.3 2.0 convolution_convert_fusion.1
  275.6 2.8 collective-permute-start.4
  280.1 2.9 collective-permute-done.4
  283.0 1.8 collective-permute-done.6
  285.4 2.8 collective-permute-start.7
  289.7 2.0 collective-permute-done.9
  291.7 1.9 collective-permute-done.8
  295.2 2.1 collective-permute-done.12
  299.6 2.9 collective-permute-start.15
  303.4 5.6 %collective-permute-done.13 = bf16[96,640]{1,0:T(8,128)(2,1)S(1)} collective-permute-done((bf16[96,640]{1,0:T(8,128)(2,1)S(1)}, bf16[96,640]{1,0:T(8,128)(2,1)S(1)}, u32[]{:S(2)}, u32[]{:S(2)}) %collective-permute-start.13) | collective-permute-done | bytes 122912 | tf_op jit(solution)/shard_map/cond/branch_1_fun/ppermute | solution.py:31
  310.7 2.4 collective-permute-start.23
  314.2 25.0 %collective-permute-done.23.a = bf16[256,768]{1,0:T(8,128)(2,1)S(1)} collective-permute-done((bf16[256,768]{1,0:T(8,128)(2,1)S(1)}, bf16[256,768]{1,0:T(8,128)(2,1)S(1)}, u32[]{:S(2)}, u32[]{:S(2)}) %collective-permute-start.23) | collective-permute-done | bytes 393248 | tf_op jit(solution)/shard_map/cond/branch_1_fun/ppermute | solution.py:31
  340.1 9.0 %collective-permute-start.19 = (bf16[384,640]{1,0:T(8,128)(2,1)S(1)}, bf16[384,640]{1,0:T(8,128)(2,1)S(1)}, u32[]{:S(2)}, u32[]{:S(2)}) collective-permute-start(bf16[384,640]{1,0:T(8,128)(2,1)S(1)} %constant_dynamic-update-slice_fusion.19.refs_0_), channel_id=1, source_target_pairs={{0,4},{4,0},{1,5},{5,1},{2,6},{6,2},{3,7},{7,3},{8,12},{12,8},{9,1... | collective-permute-start | bytes 1474568 | tf_op jit(solution)/shard_map/cond/branch_1_fun/ppermute | solution.py:35
  350.5 9.5 %collective-permute-done.25.c = bf16[256,768]{1,0:T(8,128)(2,1)} collective-permute-done((bf16[256,768]{1,0:T(8,128)(2,1)}, bf16[256,768]{1,0:T(8,128)(2,1)}, u32[]{:S(2)}, u32[]{:S(2)}) %collective-permute-start.25) | collective-permute-done | bytes 393248 | tf_op jit(solution)/shard_map/cond/branch_1_fun/ppermute | solution.py:31
  362.0 2.9 branch_1_fun.7
  364.9 8.2 %branch_1_fun.6 = (f32[768,2304]{1,0:T(8,128)}, f32[768,256]{1,0:T(8,128)S(1)}) custom-call(s32[4]{0:T(128)S(1)} %pad_add_fusion.place, bf16[384,640]{1,0:T(8,128)(2,1)S(1)} %constant_dynamic-update-slice_fusion.19.refs_0_, bf16[384,640]{1,0:T(8,128)(2,1)S(1)} %collective-permute-done.16.refs_1_, bf16[384,640]{1,0:T(8,128)(2,1)S(1)} %collective-permute-done.17.refs_2_, ...), custom_call_target="tpu_custom_call" | custom-call | tf_op jit(solution)/shard_map/cond/branch_1_fun/pallas_call | solution.py:103
  376.1 40.0 %all-reduce.5.cloned.1.call-done = (bf16[384,1152]{1,0:T(8,128)(2,1)}, bf16[384,384]{1,0:T(8,128)(2,1)}, bf16[384,1536]{1,0:T(8,128)(2,1)}, bf16[1536,384]{1,0:T...) async-done(((bf16[384,1152]{1,0:T(8,128)(2,1)}, bf16[384,384]{1,0:T(8,128)(2,1)}, ...) | async-done | bytes 14745616 | tf_op jit(solution)/shard_map/psum | solution.py:1104
  416.1 16.4 %shard_map.529 = (f32[384,1152]{1,0:T(8,128)}, f32[384,384]{1,0:T(8,128)}, f32[384,1536]{1,0:T(8,128)}, f32[1536,384]{1,0:T(8,128)}, f32[768,768]{1,0:T(8,128)},...) custom-call(bf16[384,1152]{1,0:T(8,128)(2,1)} %get-tuple-element.381.refs_0_, ...), custom_call_target="tpu_custom_call" | custom-call | bytes 44236800 | tf_op jit(solution)/shard_map/pallas_call | solution.py:860
  (339 shorter events, 64.4 us)
Async XLA Ops:
  7.2 83.2 %all-gather.2.cloned.1.call-start = ((), (), s32[]{:S(2)}) async-start(), calls=%async_computation | async-start | bytes 10948608 | tf_op jit(solution)/shard_map/all_gather | solution.py:939
  15.1 401.0 %all-reduce.5.cloned.1.call-start = ((), (), s32[]{:S(2)}) async-start(), calls=%async_computation.1 | async-start | bytes 29491200 | tf_op jit(solution)/shard_map/psum | solution.py:1104
  15.2 14.9 %collective-permute-start.26 = (bf16[352,768]{1,0:T(8,128)(2,1)S(1)}, bf16[352,768]{1,0:T(8,128)(2,1)S(1)}, u32[]{:S(2)}, u32[]{:S(2)}) collective-permute-start(bf16[352,768]{1,0:T(8,128)(2,1)S(1)} %get-tuple-element.231), channel_id=1, source_target_pairs={{0,1},{1,2},{2,3},{3,0},{4,5},{5,6},{6,7},{7,4},{8,9},{9,10},{10,1... | collective-permute-start | bytes 1622024 | tf_op jit(solution)/shard_map/ppermute | solution.py:31
  17.3 36.2 %copy-start.30 = (bf16[1,256,768]{2,1,0:T(8,128)(2,1)S(1)}, bf16[1,256,768]{2,1,0:T(8,128)(2,1)}, u32[]{:S(2)}) copy-start(bf16[1,256,768]{2,1,0:T(8,128)(2,1)} %param.36) | copy-start | bytes 1179652
  17.3 31.1 %collective-permute-start.27 = (bf16[352,768]{1,0:T(8,128)(2,1)S(1)}, bf16[352,768]{1,0:T(8,128)(2,1)}, u32[]{:S(2)}, u32[]{:S(2)}) collective-permute-start(bf16[352,768]{1,0:T(8,128)(2,1)S(1)} %get-tuple-element.232), channel_id=1, source_target_pairs={{0,2},{1,3},{2,0},{3,1},{4,6},{5,7},{6,4},{7,5},{8,10},{9,11},{10,... | collective-permute-start | bytes 1622024 | tf_op jit(solution)/shard_map/ppermute | solution.py:31
  19.7 29.6 %collective-permute-start.28 = (bf16[352,768]{1,0:T(8,128)(2,1)S(1)}, bf16[352,768]{1,0:T(8,128)(2,1)}, u32[]{:S(2)}, u32[]{:S(2)}) collective-permute-start(bf16[352,768]{1,0:T(8,128)(2,1)S(1)} %get-tuple-element.233), channel_id=1, source_target_pairs={{0,3},{1,0},{2,1},{3,2},{4,7},{5,4},{6,5},{7,6},{8,11},{9,8},{10,9... | collective-permute-start | bytes 1622024 | tf_op jit(solution)/shard_map/ppermute | solution.py:31
  24.4 66.0 %copy-start.34 = (f32[1,14208]{1,0:T(1,128)}, f32[1,14208]{1,0:T(1,128)S(1)}, u32[]{:S(2)}) copy-start(f32[1,14208]{1,0:T(1,128)S(1)} %convert_element_type.92.refs_6_.refs_10_.refs_8_.vec.refs_15_) | copy-start | bytes 170500
  50.3 3.1 collective-permute-start.29
  65.8 8.2 %collective-permute-start.32 = (bf16[256,192]{1,0:T(8,128)(2,1)S(1)}, bf16[256,192]{1,0:T(8,128)(2,1)S(1)}, u32[]{:S(2)}, u32[]{:S(2)}) collective-permute-start(bf16[256,192]{1,0:T(8,128)(2,1)S(1)} %get-tuple-element.407), channel_id=1, source_target_pairs={{0,3},{1,0},{2,1},{3,2},{4,7},{5,4},{6,5},{7,6},{8,11},{9,8},{10,9... | collective-permute-start | bytes 294920 | tf_op jit(solution)/shard_map/ppermute | solution.py:31
  66.7 9.4 %collective-permute-start.31 = (bf16[256,192]{1,0:T(8,128)(2,1)S(1)}, bf16[256,192]{1,0:T(8,128)(2,1)S(1)}, u32[]{:S(2)}, u32[]{:S(2)}) collective-permute-start(bf16[256,192]{1,0:T(8,128)(2,1)S(1)} %get-tuple-element.408), channel_id=1, source_target_pairs={{0,2},{1,3},{2,0},{3,1},{4,6},{5,7},{6,4},{7,5},{8,10},{9,11},{10,... | collective-permute-start | bytes 294920 | tf_op jit(solution)/shard_map/ppermute | solution.py:31
  67.6 12.1 %collective-permute-start.30 = (bf16[256,192]{1,0:T(8,128)(2,1)S(1)}, bf16[256,192]{1,0:T(8,128)(2,1)S(1)}, u32[]{:S(2)}, u32[]{:S(2)}) collective-permute-start(bf16[256,192]{1,0:T(8,128)(2,1)S(1)} %get-tuple-element.409), channel_id=1, source_target_pairs={{0,1},{1,2},{2,3},{3,0},{4,5},{5,6},{6,7},{7,4},{8,9},{9,10},{10,1... | collective-permute-start | bytes 294920 | tf_op jit(solution)/shard_map/ppermute | solution.py:31
  106.4 5.5 %collective-permute-start.33 = (bf16[64,384]{1,0:T(8,128)(2,1)S(1)}, bf16[64,384]{1,0:T(8,128)(2,1)S(1)}, u32[]{:S(2)}, u32[]{:S(2)}) collective-permute-start(bf16[64,384]{1,0:T(8,128)(2,1)S(1)} %get-tuple-element.238), channel_id=1, source_target_pairs={{0,1},{1,2},{2,3},{3,0},{4,5},{5,6},{6,7},{7,4},{8,9},{9,10},{10,1... | collective-permute-start | bytes 147464 | tf_op jit(solution)/shard_map/ppermute | solution.py:31
  106.4 5.5 %collective-permute-start.34 = (bf16[64,384]{1,0:T(8,128)(2,1)S(1)}, bf16[64,384]{1,0:T(8,128)(2,1)S(1)}, u32[]{:S(2)}, u32[]{:S(2)}) collective-permute-start(bf16[64,384]{1,0:T(8,128)(2,1)S(1)} %get-tuple-element.239), channel_id=1, source_target_pairs={{0,2},{1,3},{2,0},{3,1},{4,6},{5,7},{6,4},{7,5},{8,10},{9,11},{10,... | collective-permute-start | bytes 147464 | tf_op jit(solution)/shard_map/ppermute | solution.py:31
  108.1 3.8 collective-permute-start.35
  166.8 38.3 %copy-start.8 = (bf16[384,1152]{1,0:T(8,128)(2,1)S(1)}, bf16[384,1152]{1,0:T(8,128)(2,1)}, u32[]{:S(2)}) copy-start(bf16[384,1152]{1,0:T(8,128)(2,1)} %weight.3) | copy-start | bytes 2654212
  212.6 4.1 collective-permute-start.36
  215.1 4.5 %collective-permute-start.37 = (bf16[64,384]{1,0:T(8,128)(2,1)S(1)}, bf16[64,384]{1,0:T(8,128)(2,1)S(1)}, u32[]{:S(2)}, u32[]{:S(2)}) collective-permute-start(bf16[64,384]{1,0:T(8,128)(2,1)S(1)} %get-tuple-element.256), channel_id=1, source_target_pairs={{0,2},{1,3},{2,0},{3,1},{4,6},{5,7},{6,4},{7,5},{8,10},{9,11},{10,... | collective-permute-start | bytes 147464 | tf_op jit(solution)/shard_map/ppermute | solution.py:31
  215.7 4.4 collective-permute-start.38
  232.3 6.5 %collective-permute-start.39 = (bf16[256,192]{1,0:T(8,128)(2,1)S(1)}, bf16[256,192]{1,0:T(8,128)(2,1)S(1)}, u32[]{:S(2)}, u32[]{:S(2)}) collective-permute-start(bf16[256,192]{1,0:T(8,128)(2,1)S(1)} %get-tuple-element.268), channel_id=1, source_target_pairs={{0,1},{1,2},{2,3},{3,0},{4,5},{5,6},{6,7},{7,4},{8,9},{9,10},{10,1... | collective-permute-start | bytes 294920 | tf_op jit(solution)/shard_map/ppermute | solution.py:31
  232.3 6.4 %collective-permute-start.40 = (bf16[256,192]{1,0:T(8,128)(2,1)S(1)}, bf16[256,192]{1,0:T(8,128)(2,1)S(1)}, u32[]{:S(2)}, u32[]{:S(2)}) collective-permute-start(bf16[256,192]{1,0:T(8,128)(2,1)S(1)} %get-tuple-element.269), channel_id=1, source_target_pairs={{0,2},{1,3},{2,0},{3,1},{4,6},{5,7},{6,4},{7,5},{8,10},{9,11},{10,... | collective-permute-start | bytes 294920 | tf_op jit(solution)/shard_map/ppermute | solution.py:31
  233.8 5.6 %collective-permute-start.41 = (bf16[256,192]{1,0:T(8,128)(2,1)S(1)}, bf16[256,192]{1,0:T(8,128)(2,1)S(1)}, u32[]{:S(2)}, u32[]{:S(2)}) collective-permute-start(bf16[256,192]{1,0:T(8,128)(2,1)S(1)} %get-tuple-element.270), channel_id=1, source_target_pairs={{0,3},{1,0},{2,1},{3,2},{4,7},{5,4},{6,5},{7,6},{8,11},{9,8},{10,9... | collective-permute-start | bytes 294920 | tf_op jit(solution)/shard_map/ppermute | solution.py:31
  257.5 5.2 %collective-permute-start.2 = (f32[112,128]{1,0:T(8,128)S(1)}, f32[112,128]{1,0:T(8,128)S(1)}, u32[]{:S(2)}, u32[]{:S(2)}) collective-permute-start(f32[112,128]{1,0:T(8,128)S(1)} %bitcast.55), channel_id=1, source_target_pairs={{0,3},{1,0},{2,1},{3,2},{4,7},{5,4},{6,5},{7,6},{8,11},{9,8},{10,9... | collective-permute-start | bytes 172040 | tf_op jit(solution)/shard_map/cond/branch_1_fun/ppermute | solution.py:31
  259.9 5.1 %collective-permute-start.1 = (f32[112,128]{1,0:T(8,128)S(1)}, f32[112,128]{1,0:T(8,128)S(1)}, u32[]{:S(2)}, u32[]{:S(2)}) collective-permute-start(f32[112,128]{1,0:T(8,128)S(1)} %bitcast.56), channel_id=1, source_target_pairs={{0,2},{1,3},{2,0},{3,1},{4,6},{5,7},{6,4},{7,5},{8,10},{9,11},{10,... | collective-permute-start | bytes 172040 | tf_op jit(solution)/shard_map/cond/branch_1_fun/ppermute | solution.py:31
  259.9 5.8 %collective-permute-start = (f32[112,128]{1,0:T(8,128)S(1)}, f32[112,128]{1,0:T(8,128)}, u32[]{:S(2)}, u32[]{:S(2)}) collective-permute-start(f32[112,128]{1,0:T(8,128)S(1)} %bitcast.57), channel_id=1, source_target_pairs={{0,1},{1,2},{2,3},{3,0},{4,5},{5,6},{6,7},{7,4},{8,9},{9,10},{10,1... | collective-permute-start | bytes 172040 | tf_op jit(solution)/shard_map/cond/branch_1_fun/ppermute | solution.py:31
  267.0 8.3 %collective-permute-start.3 = (bf16[384,640]{1,0:T(8,128)(2,1)S(1)}, bf16[384,640]{1,0:T(8,128)(2,1)S(1)}, u32[]{:S(2)}, u32[]{:S(2)}) collective-permute-start(bf16[384,640]{1,0:T(8,128)(2,1)S(1)} %pad_maximum_fusion), channel_id=1, source_target_pairs={{0,4},{4,0},{1,5},{5,1},{2,6},{6,2},{3,7},{7,3},{8,12},{12,8},{9,1... | collective-permute-start | bytes 1474568 | tf_op jit(solution)/shard_map/cond/branch_1_fun/ppermute | solution.py:35
  275.6 84.4 %copy-start.38 = (f32[1,14208]{1,0:T(1,128)S(1)}, f32[1,14208]{1,0:T(1,128)}, u32[]{:S(2)}) copy-start(f32[1,14208]{1,0:T(1,128)} %copy-done.37) | copy-start | bytes 170500 | tf_op jit(solution)/shard_map/cond
  275.6 7.4 %collective-permute-start.4 = (bf16[96,640]{1,0:T(8,128)(2,1)S(1)}, bf16[96,640]{1,0:T(8,128)(2,1)S(1)}, u32[]{:S(2)}, u32[]{:S(2)}) collective-permute-start(bf16[96,640]{1,0:T(8,128)(2,1)S(1)} %get-tuple-element.391), channel_id=1, source_target_pairs={{0,16},{8,24},{16,0},{24,8},{1,17},{9,25},{17,1},{25,9},{2,18},{10... | collective-permute-start | bytes 368648 | tf_op jit(solution)/shard_map/cond/branch_1_fun/ppermute | solution.py:31
  278.4 6.4 %collective-permute-start.6 = (bf16[96,640]{1,0:T(8,128)(2,1)S(1)}, bf16[96,640]{1,0:T(8,128)(2,1)S(1)}, u32[]{:S(2)}, u32[]{:S(2)}) collective-permute-start(bf16[96,640]{1,0:T(8,128)(2,1)S(1)} %get-tuple-element.392), channel_id=1, source_target_pairs={{0,24},{8,0},{16,8},{24,16},{1,25},{9,1},{17,9},{25,17},{2,26},{10... | collective-permute-start | bytes 368648 | tf_op jit(solution)/shard_map/cond/branch_1_fun/ppermute | solution.py:31
  279.4 5.9 %collective-permute-start.5 = (bf16[96,640]{1,0:T(8,128)(2,1)S(1)}, bf16[96,640]{1,0:T(8,128)(2,1)S(1)}, u32[]{:S(2)}, u32[]{:S(2)}) collective-permute-start(bf16[96,640]{1,0:T(8,128)(2,1)S(1)} %get-tuple-element.393), channel_id=1, source_target_pairs={{0,8},{8,16},{16,24},{24,0},{1,9},{9,17},{17,25},{25,1},{2,10},{10... | collective-permute-start | bytes 368648 | tf_op jit(solution)/shard_map/cond/branch_1_fun/ppermute | solution.py:31
  285.4 4.3 collective-permute-start.7
  288.1 3.6 collective-permute-start.9
  288.9 4.7 %collective-permute-start.8 = (bf16[24,640]{1,0:T(8,128)(2,1)S(1)}, bf16[24,640]{1,0:T(8,128)(2,1)S(1)}, u32[]{:S(2)}, u32[]{:S(2)}) collective-permute-start(bf16[24,640]{1,0:T(8,128)(2,1)S(1)} %get-tuple-element.402), channel_id=1, source_target_pairs={{0,32},{32,64},{64,96},{96,0},{1,33},{33,65},{65,97},{97,1},{2,34}... | collective-permute-start | bytes 92168 | tf_op jit(solution)/shard_map/cond/branch_1_fun/ppermute | solution.py:31
  293.7 3.7 collective-permute-start.12
  293.7 4.8 %collective-permute-start.11 = (bf16[24,640]{1,0:T(8,128)(2,1)S(1)}, bf16[24,640]{1,0:T(8,128)(2,1)S(1)}, u32[]{:S(2)}, u32[]{:S(2)}) collective-permute-start(bf16[24,640]{1,0:T(8,128)(2,1)S(1)} %get-tuple-element.390), channel_id=1, source_target_pairs={{0,64},{32,96},{64,0},{96,32},{1,65},{33,97},{65,1},{97,33},{2,66}... | collective-permute-start | bytes 92168 | tf_op jit(solution)/shard_map/cond/branch_1_fun/ppermute | solution.py:31
  295.2 4.5 %collective-permute-start.10 = (bf16[24,640]{1,0:T(8,128)(2,1)S(1)}, bf16[24,640]{1,0:T(8,128)(2,1)S(1)}, u32[]{:S(2)}, u32[]{:S(2)}) collective-permute-start(bf16[24,640]{1,0:T(8,128)(2,1)S(1)} %get-tuple-element.390), channel_id=1, source_target_pairs={{0,32},{32,64},{64,96},{96,0},{1,33},{33,65},{65,97},{97,1},{2,34}... | collective-permute-start | bytes 92168 | tf_op jit(solution)/shard_map/cond/branch_1_fun/ppermute | solution.py:31
  299.6 9.4 %collective-permute-start.15 = (bf16[96,640]{1,0:T(8,128)(2,1)S(1)}, bf16[96,640]{1,0:T(8,128)(2,1)S(1)}, u32[]{:S(2)}, u32[]{:S(2)}) collective-permute-start(bf16[96,640]{1,0:T(8,128)(2,1)S(1)} %pad_maximum_fusion.1), channel_id=1, source_target_pairs={{0,24},{8,0},{16,8},{24,16},{1,25},{9,1},{17,9},{25,17},{2,26},{10... | collective-permute-start | bytes 368648 | tf_op jit(solution)/shard_map/cond/branch_1_fun/ppermute | solution.py:31
  302.5 6.5 %collective-permute-start.14 = (bf16[96,640]{1,0:T(8,128)(2,1)S(1)}, bf16[96,640]{1,0:T(8,128)(2,1)S(1)}, u32[]{:S(2)}, u32[]{:S(2)}) collective-permute-start(bf16[96,640]{1,0:T(8,128)(2,1)S(1)} %pad_maximum_fusion.1), channel_id=1, source_target_pairs={{0,16},{8,24},{16,0},{24,8},{1,17},{9,25},{17,1},{25,9},{2,18},{10... | collective-permute-start | bytes 368648 | tf_op jit(solution)/shard_map/cond/branch_1_fun/ppermute | solution.py:31
  302.8 6.3 %collective-permute-start.13 = (bf16[96,640]{1,0:T(8,128)(2,1)S(1)}, bf16[96,640]{1,0:T(8,128)(2,1)S(1)}, u32[]{:S(2)}, u32[]{:S(2)}) collective-permute-start(bf16[96,640]{1,0:T(8,128)(2,1)S(1)} %pad_maximum_fusion.1), channel_id=1, source_target_pairs={{0,8},{8,16},{16,24},{24,0},{1,9},{9,17},{17,25},{25,1},{2,10},{10... | collective-permute-start | bytes 368648 | tf_op jit(solution)/shard_map/cond/branch_1_fun/ppermute | solution.py:31
  309.1 39.9 %collective-permute-start.18 = (bf16[384,640]{1,0:T(8,128)(2,1)S(1)}, bf16[384,640]{1,0:T(8,128)(2,1)S(1)}, u32[]{:S(2)}, u32[]{:S(2)}) collective-permute-start(bf16[384,640]{1,0:T(8,128)(2,1)S(1)} %constant_dynamic-update-slice_fusion.19.refs_0_), channel_id=1, source_target_pairs={{0,3},{1,0},{2,1},{3,2},{4,7},{5,4},{6,5},{7,6},{8,11},{9,8},{10,9... | collective-permute-start | bytes 1474568 | tf_op jit(solution)/shard_map/cond/branch_1_fun/ppermute | solution.py:31
  309.3 39.8 %collective-permute-start.17 = (bf16[384,640]{1,0:T(8,128)(2,1)S(1)}, bf16[384,640]{1,0:T(8,128)(2,1)S(1)}, u32[]{:S(2)}, u32[]{:S(2)}) collective-permute-start(bf16[384,640]{1,0:T(8,128)(2,1)S(1)} %constant_dynamic-update-slice_fusion.19.refs_0_), channel_id=1, source_target_pairs={{0,2},{1,3},{2,0},{3,1},{4,6},{5,7},{6,4},{7,5},{8,10},{9,11},{10,... | collective-permute-start | bytes 1474568 | tf_op jit(solution)/shard_map/cond/branch_1_fun/ppermute | solution.py:31
  309.9 39.7 %collective-permute-start.16 = (bf16[384,640]{1,0:T(8,128)(2,1)S(1)}, bf16[384,640]{1,0:T(8,128)(2,1)S(1)}, u32[]{:S(2)}, u32[]{:S(2)}) collective-permute-start(bf16[384,640]{1,0:T(8,128)(2,1)S(1)} %constant_dynamic-update-slice_fusion.19.refs_0_), channel_id=1, source_target_pairs={{0,1},{1,2},{2,3},{3,0},{4,5},{5,6},{6,7},{7,4},{8,9},{9,10},{10,1... | collective-permute-start | bytes 1474568 | tf_op jit(solution)/shard_map/cond/branch_1_fun/ppermute | solution.py:31
  310.7 28.6 %collective-permute-start.23 = (bf16[256,768]{1,0:T(8,128)(2,1)S(1)}, bf16[256,768]{1,0:T(8,128)(2,1)S(1)}, u32[]{:S(2)}, u32[]{:S(2)}) collective-permute-start(bf16[256,768]{1,0:T(8,128)(2,1)S(1)} %get-tuple-element.124), channel_id=1, source_target_pairs={{0,3},{1,0},{2,1},{3,2},{4,7},{5,4},{6,5},{7,6},{8,11},{9,8},{10,9... | collective-permute-start | bytes 1179656 | tf_op jit(solution)/shard_map/cond/branch_1_fun/ppermute | solution.py:31
  313.1 36.6 %collective-permute-start.24 = (bf16[256,768]{1,0:T(8,128)(2,1)}, bf16[256,768]{1,0:T(8,128)(2,1)S(1)}, u32[]{:S(2)}, u32[]{:S(2)}) collective-permute-start(bf16[256,768]{1,0:T(8,128)(2,1)} %get-tuple-element.125), channel_id=1, source_target_pairs={{0,2},{1,3},{2,0},{3,1},{4,6},{5,7},{6,4},{7,5},{8,10},{9,11},{10,... | collective-permute-start | bytes 1179656 | tf_op jit(solution)/shard_map/cond/branch_1_fun/ppermute | solution.py:31
  340.1 24.8 %collective-permute-start.19 = (bf16[384,640]{1,0:T(8,128)(2,1)S(1)}, bf16[384,640]{1,0:T(8,128)(2,1)S(1)}, u32[]{:S(2)}, u32[]{:S(2)}) collective-permute-start(bf16[384,640]{1,0:T(8,128)(2,1)S(1)} %constant_dynamic-update-slice_fusion.19.refs_0_), channel_id=1, source_target_pairs={{0,4},{4,0},{1,5},{5,1},{2,6},{6,2},{3,7},{7,3},{8,12},{12,8},{9,1... | collective-permute-start | bytes 1474568 | tf_op jit(solution)/shard_map/cond/branch_1_fun/ppermute | solution.py:35
  349.1 15.8 %collective-permute-start.22 = (bf16[384,640]{1,0:T(8,128)(2,1)S(1)}, bf16[384,640]{1,0:T(8,128)(2,1)}, u32[]{:S(2)}, u32[]{:S(2)}) collective-permute-start(bf16[384,640]{1,0:T(8,128)(2,1)S(1)} %collective-permute-done.18.refs_3_), channel_id=1, source_target_pairs={{0,4},{4,0},{1,5},{5,1},{2,6},{6,2},{3,7},{7,3},{8,12},{12,8},{9,1... | collective-permute-start | bytes 1474568 | tf_op jit(solution)/shard_map/cond/branch_1_fun/ppermute | solution.py:35
  349.1 15.8 %collective-permute-start.21 = (bf16[384,640]{1,0:T(8,128)(2,1)S(1)}, bf16[384,640]{1,0:T(8,128)(2,1)}, u32[]{:S(2)}, u32[]{:S(2)}) collective-permute-start(bf16[384,640]{1,0:T(8,128)(2,1)S(1)} %collective-permute-done.17.refs_2_), channel_id=1, source_target_pairs={{0,4},{4,0},{1,5},{5,1},{2,6},{6,2},{3,7},{7,3},{8,12},{12,8},{9,1... | collective-permute-start | bytes 1474568 | tf_op jit(solution)/shard_map/cond/branch_1_fun/ppermute | solution.py:35
  349.6 15.3 %collective-permute-start.20 = (bf16[384,640]{1,0:T(8,128)(2,1)S(1)}, bf16[384,640]{1,0:T(8,128)(2,1)}, u32[]{:S(2)}, u32[]{:S(2)}) collective-permute-start(bf16[384,640]{1,0:T(8,128)(2,1)S(1)} %collective-permute-done.16.refs_1_), channel_id=1, source_target_pairs={{0,4},{4,0},{1,5},{5,1},{2,6},{6,2},{3,7},{7,3},{8,12},{12,8},{9,1... | collective-permute-start | bytes 1474568 | tf_op jit(solution)/shard_map/cond/branch_1_fun/ppermute | solution.py:35
  350.4 9.6 %collective-permute-start.25 = (bf16[256,768]{1,0:T(8,128)(2,1)}, bf16[256,768]{1,0:T(8,128)(2,1)}, u32[]{:S(2)}, u32[]{:S(2)}) collective-permute-start(bf16[256,768]{1,0:T(8,128)(2,1)} %copy-done.25), channel_id=1, source_target_pairs={{0,1},{1,2},{2,3},{3,0},{4,5},{5,6},{6,7},{7,4},{8,9},{9,10},{10,1... | collective-permute-start | bytes 1179656 | tf_op jit(solution)/shard_map/cond/branch_1_fun/ppermute | solution.py:31
  (80 other events, 711.6 us)
Sparse Core Ops, SparseCore 0:
  15.2 75.1 all-gather.1
  232.4 183.6 all-reduce.4

commit v2 on v1

--- a/solution.py
+++ b/solution.py
@@ -397,7 +397,7 @@
             out_specs=[whole(a) for a in outs],
         ),
         out_shape=outs,
-        compiler_params=room(24),
+        compiler_params=room(56),
     )(place, weight, inputs, fc2, proj, fc1)
 
 

time: 448 us -> 450 us (level)
  waiting for transfers between devices: 149 us -> 156 us
  local copies, waits for them, and re-layouts: 34.2 us -> 28.4 us
    ppermute x36, waiting for transfers between devices: 96.8 us -> 103 us  [shift(): return lax.ppermute(value, axis, [(i, (i + step) % 4) for i in range(4)])]
  transfers between devices with their start and end apart: 44 -> 44, of which waited for: 28 -> 27; matrix products, arithmetic and copies ran while one was open for 5% -> 4% of each run, Pallas kernels for 9% -> 9%
where the time goes in v2:
time: 450 us; the launch traced here: 444 us
  Pallas kernels  171 us (38%)
  waiting for transfers between devices  156 us (35%)
  starting transfers between devices  58.6 us (13%)
  local copies, waits for them, and re-layouts  28.4 us (6%)
  between operations  16.1 us (4%)
  matrix products  6.78 us (2%)
  other arithmetic  5.14 us (1%)
    ppermute x36, waiting for transfers between devices, shift(): return lax.ppermute(value, axis, [(i, (i + step) % 4) for i in range(4)])  103 us
    pallas_call x2, Pallas kernels, attend_back(): pl.pallas_call(functools.partial(backward_kernel, block=block, masked=mas...  50.4 us
    psum x1, waiting for transfers between devices, body(): rest_grads = lax.psum(early, ALL)  40.5 us
    ppermute x36, starting transfers between devices, shift(): return lax.ppermute(value, axis, [(i, (i + step) % 4) for i in range(4)])  39.9 us
    pallas_call x2, Pallas kernels, attend(): pl.pallas_call(functools.partial(forward_kernel, block=block, masked=mask...  29.1 us
    pallas_call x1, Pallas kernels, dec_mid(): pl.pallas_call(functools.partial(dec_mid_kernel, vectors=vectors, chunk=c...  22.2 us
    ppermute x6, starting transfers between devices, swap(): return lax.ppermute(value, 'core', [(0, 1), (1, 0)])  18.7 us
    pallas_call x1, Pallas kernels, widen(): pl.pallas_call(widen_kernel, grid=(8,), in_specs=[piece(a) for a in array...  16.4 us
  transfers between devices with their start and end apart: 44, of which 27 were waited for; matrix products, arithmetic and copies ran while one was open for 4% of the time, Pallas kernels for 9%

profile of v2, /device:TPU:1, one launch (start us, length us, event | category | flops | bytes accessed | tf_op | source)
XLA Modules:
  0.0 443.6 jit_solution(12486288542378952850)
XLA Ops:
  8.0 4.9 %shard_map.519 = (bf16[192,768]{1,0:T(8,128)(2,1)}, bf16[352,768]{1,0:T(8,128)(2,1)}, bf16[352,768]{1,0:T(8,128)(2,1)}, bf16[352,768]{1,0:T(8,128)(2,1)}, bf16[9,24,768]{2,1,0:T(8,128)(2,1)}) custom-call(s32[3]{0:T(128)} %pad_add_fusion.1.place, bf16[192,2304]{1,0:T(8,128)(2,1)} %weight.2, bf16[256,768]{1,0:T(8,128)(2,1)} %bitcast.49, bf16[768,768]{1,0:T(8,128)(2,1)} %fc2.2, ...), custom_call_target="tpu_custom_call" | custom-call | tf_op jit(solution)/shard_map/pallas_call | solution.py:391
  13.0 2.1 collective-permute-start.26
  15.1 2.5 collective-permute-start.27
  24.2 3.9 collective-permute-done.26.refs_2_
  28.1 18.2 %collective-permute-done.27.refs_3_ = bf16[352,768]{1,0:T(8,128)(2,1)S(1)} collective-permute-done((bf16[352,768]{1,0:T(8,128)(2,1)}, bf16[352,768]{1,0:T(8,128)(2,1)S(1)}, u32[]{:S(2)}, u32[]{:S(2)}) %collective-permute-start.27) | collective-permute-done | bytes 540704 | tf_op jit(solution)/shard_map/ppermute | solution.py:31
  47.2 1.7 collective-permute-start.29
  50.3 4.5 %shard_map.520 = (bf16[1024,768]{1,0:T(8,128)(2,1)S(1)}, bf16[1024,768]{1,0:T(8,128)(2,1)}, bf16[768,768]{1,0:T(8,128)(2,1)}) custom-call(s32[3]{0:T(128)S(1)} %copy-done.18, bf16[256,768]{1,0:T(8,128)(2,1)S(1)} %bitcast.51, bf16[192,768]{1,0:T(8,128)(2,1)S(1)} %copy-done.24, bf16[352,768]{1,0:T(8,128)(2,1)S(1)} %collective-permute-done.26.refs_2_, ...), custom_call_target="tpu_custom_call" | custom-call | flops 1207959552 | bytes 6291456 | tf_op jit(solution)/shard_map/pallas_call | solution.py:437
  54.9 7.7 %shard_map.521 = (bf16[1024,256]{1,0:T(8,128)(2,1)S(1)}, f32[2,1024,2]{2,1,0:T(8,128)}) custom-call(s32[1024,1]{1,0:T(8,128)S(1)} %copy.69.refs_0_, s32[1,1024]{1,0:T(1,128)S(1)} %bitcast.60, bf16[1024,768]{1,0:T(8,128)(2,1)S(1)} %get-tuple-element.234.refs_2_.refs_3_.refs_4_, bf16[1024,768]{1,0:T(8,128)(2,1)S(1)} %get-tuple-element.234.refs_2_.refs_3_.refs_4_, ...), custom_call_target="tpu_custom_call" | custom-call | flops 4294967296 | bytes 2097152 | tf_op jit(solution)/shard_map/pallas_call | solution.py:249
  65.5 5.4 %collective-permute-done.32.refs_3_ = bf16[256,192]{1,0:T(8,128)(2,1)S(1)} collective-permute-done((bf16[256,192]{1,0:T(8,128)(2,1)S(1)}, bf16[256,192]{1,0:T(8,128)(2,1)S(1)}, u32[]{:S(2)}, u32[]{:S(2)}) %collective-permute-start.32) | collective-permute-done | bytes 98336 | tf_op jit(solution)/shard_map/ppermute | solution.py:31
  70.8 2.4 collective-permute-done.31.refs_2_
  73.2 3.5 collective-permute-done.30.refs_1_
  76.7 11.8 %all-gather.2.cloned.1.call-done.refs_5_.refs_6_.refs_7_.refs_12_.refs_13_.refs_14_ = bf16[9,768,768]{2,1,0:T(8,128)(2,1)} async-done(((bf16[9,24,768]{2,1,0:T(8,128)(2,1)}), bf16[9,768,768]{2,1,0:T(8,128)(2,1)}) %all-gather.2.cloned.1.call-update) | async-done | bytes 10616848 | tf_op jit(solution)/shard_map/all_gather | solution.py:939
  88.5 4.0 copy-done
  92.6 7.6 %shard_map.522 = (bf16[256,768]{1,0:T(8,128)(2,1)S(1)}, f32[256,768]{1,0:T(8,128)S(1)}, bf16[256,768]{1,0:T(8,128)(2,1)S(1)}, bf16[256,3072]{1,0:T(8,128)(2,1)S(...) custom-call(s32[3]{0:T(128)S(1)} %copy-done.18, ...), custom_call_target="tpu_custom_call" | custom-call | flops 3019898880 | bytes 11796480 | tf_op jit(solution)/shard_map/pallas_call | solution.py:506
  104.5 1.7 collective-permute-start.34
  111.3 1.7 copy-done.25
  113.0 5.2 %shard_map.523 = (f32[1568,384]{1,0:T(8,128)S(1)}, bf16[1568,384]{1,0:T(8,128)(2,1)S(1)}, bf16[1568,1152]{1,0:T(8,128)(2,1)S(1)}) custom-call(bf16[64,384]{1,0:T(8,128)(2,1)S(1)} %get-tuple-element.237.refs_0_, bf16[64,384]{1,0:T(8,128)(2,1)S(1)} %collective-permute-done.33.refs_1_, bf16[64,384]{1,0:T(8,128)(2,1)S(1)} %collective-permute-done.34.refs_2_, ...), custom_call_target="tpu_custom_call" | custom-call | flops 1849688064 | bytes 9633792 | tf_op jit(solution)/shard_map/pallas_call | solution.py:699
  118.3 21.4 %shard_map.524 = (bf16[1568,384]{1,0:T(8,128)(2,1)S(1)}, f32[3,1568,2]{2,1,0:T(8,128)S(1)}) custom-call(bf16[1568,1152]{1,0:T(8,128)(2,1)S(1)} %get-tuple-element.242.refs_0_.refs_1_.refs_2_, bf16[1568,1152]{1,0:T(8,128)(2,1)S(1)} %get-tuple-element.242.refs_0_.refs_1_.refs_2_, bf16[1568,1152]{1,0:T(8,128)(2,1)S(1)} %get-tuple-element.242.refs_0_.refs_1_.refs_2_), custom_call_target="tpu_custom_call" | custom-call | flops 15105785856 | bytes 4816896 | tf_op jit(solution)/shard_map/pallas_call | solution.py:249
  141.1 22.2 %shard_map.525 = (bf16[1568,384]{1,0:T(8,128)(2,1)}, f32[1568,384]{1,0:T(8,128)S(1)}, bf16[1568,384]{1,0:T(8,128)(2,1)S(1)}, bf16[1568,384]{1,0:T(8,128)(2,1)S(1...) custom-call(f32[1568,384]{1,0:T(8,128)S(1)} %get-tuple-element.241.x, ...), custom_call_target="tpu_custom_call" | custom-call | flops 25895632896 | bytes 12042240 | tf_op jit(solution)/shard_map/pallas_call | solution.py:839
  163.3 1.7 copy-done.27
  165.0 38.3 %shard_map.526.grad = bf16[1568,1152]{1,0:T(8,128)(2,1)S(1)} custom-call(bf16[1568,1152]{1,0:T(8,128)(2,1)S(1)} %get-tuple-element.242.refs_0_.refs_1_.refs_2_, bf16[1568,1152]{1,0:T(8,128)(2,1)S(1)} %get-tuple-element.242.refs_0_.refs_1_.refs_2_, bf16[1568,1152]{1,0:T(8,128)(2,1)S(1)} %get-tuple-element.242.refs_0_.refs_1_.refs_2_, ...), custom_call_target="tpu_custom_call" | custom-call | flops 37764464640 | bytes 9633792 | tf_op jit(solution)/shard_map/pallas_call | solution.py:270
  203.4 5.5 %shard_map.527 = (bf16[64,384]{1,0:T(8,128)(2,1)S(1)}, bf16[64,384]{1,0:T(8,128)(2,1)S(1)}, bf16[64,384]{1,0:T(8,128)(2,1)S(1)}, bf16[64,384]{1,0:T(8,128)(2,1)S...) custom-call(bf16[1568,1152]{1,0:T(8,128)(2,1)S(1)} %shard_map.526.grad, ...), custom_call_target="tpu_custom_call" | custom-call | flops 1849688064 | bytes 9633792 | tf_op jit(solution)/shard_map/pallas_call | solution.py:742
  208.8 2.0 convolution_convert_fusion.2.refs_16_
  210.8 2.4 collective-permute-start.36
  214.8 2.9 collective-permute-done.37.refs_2_
  218.3 12.0 %shard_map.528 = (bf16[768,3072]{1,0:T(8,128)(2,1)}, bf16[3072,768]{1,0:T(8,128)(2,1)}, f32[1,3072]{1,0:T(1,128)S(1)}, f32[256,768]{1,0:T(8,128)}, bf16[768,768]...) custom-call(s32[3]{0:T(128)S(1)} %copy-done.18, ...), custom_call_target="tpu_custom_call" | custom-call | flops 6039797760 | bytes 23592960 | tf_op jit(solution)/shard_map/pallas_call | solution.py:583
  237.6 139.1 %conditional.1 = (f32[768,2304]{1,0:T(8,128)}, f32[768,256]{1,0:T(8,128)S(1)}, f32[1,256,768]{2,1,0:T(8,128)}) conditional(s32[]{:T(128)} %bitcast.22, () %tuple.21, (s32[]{:T(128)}, bf16[1024,768]{1,0:T(8,128)(2,1)}, bf16[1024,192]{1,0:T(8,128)(2,1)S(1)}, s32[1024,1]{0,1:T(1,128)S(1)}, s32[1,1024]{1,0:T(1,128)S(1)}, ...), branch_computations={%region_2.4_spmd, %region_3.5_spmd} | conditional | flops 13159375872 | bytes 71831120 | solution.py:1105
  238.0 12.1 %branch_1_fun.4.refs_4_ = bf16[1024,768]{1,0:T(8,128)(2,1)S(1)} custom-call(s32[1024,1]{1,0:T(8,128)S(1)} %copy.73.refs_0_, s32[1,1024]{1,0:T(1,128)S(1)} %get-tuple-element.83.refs_1_, bf16[1024,768]{1,0:T(8,128)(2,1)} %get-tuple-element.84.refs_2_.refs_3_.refs_4_, bf16[1024,768]{1,0:T(8,128)(2,1)} %get-tuple-element.84.refs_2_.refs_3_.refs_4_, ...), custom_call_target="tpu_custom_call" | custom-call | flops 10737418240 | bytes 4194304 | tf_op jit(solution)/shard_map/cond/branch_1_fun/pallas_call | solution.py:270
  250.3 2.4 branch_1_fun.5
  254.0 2.5 collective-permute-start.2
  257.1 2.0 convolution_convert_fusion
  259.2 2.3 collective-permute-done.1
  263.5 6.5 %collective-permute-start.3 = (bf16[384,640]{1,0:T(8,128)(2,1)S(1)}, bf16[384,640]{1,0:T(8,128)(2,1)S(1)}, u32[]{:S(2)}, u32[]{:S(2)}) collective-permute-start(bf16[384,640]{1,0:T(8,128)(2,1)S(1)} %pad_maximum_fusion), channel_id=1, source_target_pairs={{0,4},{4,0},{1,5},{5,1},{2,6},{6,2},{3,7},{7,3},{8,12},{12,8},{9,1... | collective-permute-start | bytes 1474568 | tf_op jit(solution)/shard_map/cond/branch_1_fun/ppermute | solution.py:35
  269.9 2.0 convolution_convert_fusion.1
  272.2 2.7 collective-permute-start.4
  276.7 3.2 collective-permute-done.4
  279.9 2.6 collective-permute-done.6
  283.2 2.7 collective-permute-start.7
  290.8 1.7 collective-permute-start.11
  299.1 6.7 %collective-permute-done.13 = bf16[96,640]{1,0:T(8,128)(2,1)S(1)} collective-permute-done((bf16[96,640]{1,0:T(8,128)(2,1)S(1)}, bf16[96,640]{1,0:T(8,128)(2,1)S(1)}, u32[]{:S(2)}, u32[]{:S(2)}) %collective-permute-start.13) | collective-permute-done | bytes 122912 | tf_op jit(solution)/shard_map/cond/branch_1_fun/ppermute | solution.py:31
  308.8 2.7 collective-permute-start.23
  311.8 22.7 %collective-permute-done.23.a = bf16[256,768]{1,0:T(8,128)(2,1)S(1)} collective-permute-done((bf16[256,768]{1,0:T(8,128)(2,1)S(1)}, bf16[256,768]{1,0:T(8,128)(2,1)S(1)}, u32[]{:S(2)}, u32[]{:S(2)}) %collective-permute-start.23) | collective-permute-done | bytes 393248 | tf_op jit(solution)/shard_map/cond/branch_1_fun/ppermute | solution.py:31
  335.3 9.9 %collective-permute-start.19 = (bf16[384,640]{1,0:T(8,128)(2,1)S(1)}, bf16[384,640]{1,0:T(8,128)(2,1)S(1)}, u32[]{:S(2)}, u32[]{:S(2)}) collective-permute-start(bf16[384,640]{1,0:T(8,128)(2,1)S(1)} %constant_dynamic-update-slice_fusion.19.refs_0_), channel_id=1, source_target_pairs={{0,4},{4,0},{1,5},{5,1},{2,6},{6,2},{3,7},{7,3},{8,12},{12,8},{9,1... | collective-permute-start | bytes 1474568 | tf_op jit(solution)/shard_map/cond/branch_1_fun/ppermute | solution.py:35
  346.9 16.4 %collective-permute-done.25.c = bf16[256,768]{1,0:T(8,128)(2,1)} collective-permute-done((bf16[256,768]{1,0:T(8,128)(2,1)}, bf16[256,768]{1,0:T(8,128)(2,1)}, u32[]{:S(2)}, u32[]{:S(2)}) %collective-permute-start.25) | collective-permute-done | bytes 393248 | tf_op jit(solution)/shard_map/cond/branch_1_fun/ppermute | solution.py:31
  365.3 2.9 branch_1_fun.7
  368.1 8.2 %branch_1_fun.6 = (f32[768,2304]{1,0:T(8,128)}, f32[768,256]{1,0:T(8,128)S(1)}) custom-call(s32[4]{0:T(128)S(1)} %pad_add_fusion.place, bf16[384,640]{1,0:T(8,128)(2,1)S(1)} %constant_dynamic-update-slice_fusion.19.refs_0_, bf16[384,640]{1,0:T(8,128)(2,1)S(1)} %collective-permute-done.16.refs_1_, bf16[384,640]{1,0:T(8,128)(2,1)S(1)} %collective-permute-done.17.refs_2_, ...), custom_call_target="tpu_custom_call" | custom-call | tf_op jit(solution)/shard_map/cond/branch_1_fun/pallas_call | solution.py:103
  379.3 40.5 %all-reduce.5.cloned.1.call-done = (bf16[384,1152]{1,0:T(8,128)(2,1)}, bf16[384,384]{1,0:T(8,128)(2,1)}, bf16[384,1536]{1,0:T(8,128)(2,1)}, bf16[1536,384]{1,0:T...) async-done(((bf16[384,1152]{1,0:T(8,128)(2,1)}, bf16[384,384]{1,0:T(8,128)(2,1)}, ...) | async-done | bytes 14745616 | tf_op jit(solution)/shard_map/psum | solution.py:1104
  419.9 16.4 %shard_map.529 = (f32[384,1152]{1,0:T(8,128)}, f32[384,384]{1,0:T(8,128)}, f32[384,1536]{1,0:T(8,128)}, f32[1536,384]{1,0:T(8,128)}, f32[768,768]{1,0:T(8,128)},...) custom-call(bf16[384,1152]{1,0:T(8,128)(2,1)} %get-tuple-element.381.refs_0_, ...), custom_call_target="tpu_custom_call" | custom-call | bytes 44236800 | tf_op jit(solution)/shard_map/pallas_call | solution.py:860
  (343 shorter events, 60.4 us)
Async XLA Ops:
  7.2 81.3 %all-gather.2.cloned.1.call-start = ((), (), s32[]{:S(2)}) async-start(), calls=%async_computation | async-start | bytes 10948608 | tf_op jit(solution)/shard_map/all_gather | solution.py:939
  13.0 406.9 %all-reduce.5.cloned.1.call-start = ((), (), s32[]{:S(2)}) async-start(), calls=%async_computation.1 | async-start | bytes 29491200 | tf_op jit(solution)/shard_map/psum | solution.py:1104
  13.0 15.1 %collective-permute-start.26 = (bf16[352,768]{1,0:T(8,128)(2,1)}, bf16[352,768]{1,0:T(8,128)(2,1)S(1)}, u32[]{:S(2)}, u32[]{:S(2)}) collective-permute-start(bf16[352,768]{1,0:T(8,128)(2,1)} %get-tuple-element.231), channel_id=1, source_target_pairs={{0,1},{1,2},{2,3},{3,0},{4,5},{5,6},{6,7},{7,4},{8,9},{9,10},{10,1... | collective-permute-start | bytes 1622024 | tf_op jit(solution)/shard_map/ppermute | solution.py:31
  15.1 35.2 %copy-start.28 = (bf16[1,256,768]{2,1,0:T(8,128)(2,1)S(1)}, bf16[1,256,768]{2,1,0:T(8,128)(2,1)}, u32[]{:S(2)}) copy-start(bf16[1,256,768]{2,1,0:T(8,128)(2,1)} %param.36) | copy-start | bytes 1179652
  15.1 31.2 %collective-permute-start.27 = (bf16[352,768]{1,0:T(8,128)(2,1)}, bf16[352,768]{1,0:T(8,128)(2,1)S(1)}, u32[]{:S(2)}, u32[]{:S(2)}) collective-permute-start(bf16[352,768]{1,0:T(8,128)(2,1)} %get-tuple-element.232), channel_id=1, source_target_pairs={{0,2},{1,3},{2,0},{3,1},{4,6},{5,7},{6,4},{7,5},{8,10},{9,11},{10,... | collective-permute-start | bytes 1622024 | tf_op jit(solution)/shard_map/ppermute | solution.py:31
  17.6 28.8 %collective-permute-start.28 = (bf16[352,768]{1,0:T(8,128)(2,1)}, bf16[352,768]{1,0:T(8,128)(2,1)S(1)}, u32[]{:S(2)}, u32[]{:S(2)}) collective-permute-start(bf16[352,768]{1,0:T(8,128)(2,1)} %get-tuple-element.233), channel_id=1, source_target_pairs={{0,3},{1,0},{2,1},{3,2},{4,7},{5,4},{6,5},{7,6},{8,11},{9,8},{10,9... | collective-permute-start | bytes 1622024 | tf_op jit(solution)/shard_map/ppermute | solution.py:31
  22.3 66.3 %copy-start.32 = (f32[1,14208]{1,0:T(1,128)}, f32[1,14208]{1,0:T(1,128)S(1)}, u32[]{:S(2)}) copy-start(f32[1,14208]{1,0:T(1,128)S(1)} %convert_element_type.92.refs_6_.refs_10_.refs_8_.vec.refs_15_) | copy-start | bytes 170500
  47.2 3.1 collective-permute-start.29
  62.6 8.2 %collective-permute-start.32 = (bf16[256,192]{1,0:T(8,128)(2,1)S(1)}, bf16[256,192]{1,0:T(8,128)(2,1)S(1)}, u32[]{:S(2)}, u32[]{:S(2)}) collective-permute-start(bf16[256,192]{1,0:T(8,128)(2,1)S(1)} %get-tuple-element.407), channel_id=1, source_target_pairs={{0,3},{1,0},{2,1},{3,2},{4,7},{5,4},{6,5},{7,6},{8,11},{9,8},{10,9... | collective-permute-start | bytes 294920 | tf_op jit(solution)/shard_map/ppermute | solution.py:31
  63.8 9.4 %collective-permute-start.31 = (bf16[256,192]{1,0:T(8,128)(2,1)S(1)}, bf16[256,192]{1,0:T(8,128)(2,1)S(1)}, u32[]{:S(2)}, u32[]{:S(2)}) collective-permute-start(bf16[256,192]{1,0:T(8,128)(2,1)S(1)} %get-tuple-element.408), channel_id=1, source_target_pairs={{0,2},{1,3},{2,0},{3,1},{4,6},{5,7},{6,4},{7,5},{8,10},{9,11},{10,... | collective-permute-start | bytes 294920 | tf_op jit(solution)/shard_map/ppermute | solution.py:31
  64.7 12.1 %collective-permute-start.30 = (bf16[256,192]{1,0:T(8,128)(2,1)S(1)}, bf16[256,192]{1,0:T(8,128)(2,1)S(1)}, u32[]{:S(2)}, u32[]{:S(2)}) collective-permute-start(bf16[256,192]{1,0:T(8,128)(2,1)S(1)} %get-tuple-element.409), channel_id=1, source_target_pairs={{0,1},{1,2},{2,3},{3,0},{4,5},{5,6},{6,7},{7,4},{8,9},{9,10},{10,1... | collective-permute-start | bytes 294920 | tf_op jit(solution)/shard_map/ppermute | solution.py:31
  104.5 5.7 %collective-permute-start.33 = (bf16[64,384]{1,0:T(8,128)(2,1)S(1)}, bf16[64,384]{1,0:T(8,128)(2,1)S(1)}, u32[]{:S(2)}, u32[]{:S(2)}) collective-permute-start(bf16[64,384]{1,0:T(8,128)(2,1)S(1)} %get-tuple-element.238), channel_id=1, source_target_pairs={{0,1},{1,2},{2,3},{3,0},{4,5},{5,6},{6,7},{7,4},{8,9},{9,10},{10,1... | collective-permute-start | bytes 147464 | tf_op jit(solution)/shard_map/ppermute | solution.py:31
  104.5 5.7 %collective-permute-start.34 = (bf16[64,384]{1,0:T(8,128)(2,1)S(1)}, bf16[64,384]{1,0:T(8,128)(2,1)S(1)}, u32[]{:S(2)}, u32[]{:S(2)}) collective-permute-start(bf16[64,384]{1,0:T(8,128)(2,1)S(1)} %get-tuple-element.239), channel_id=1, source_target_pairs={{0,2},{1,3},{2,0},{3,1},{4,6},{5,7},{6,4},{7,5},{8,10},{9,11},{10,... | collective-permute-start | bytes 147464 | tf_op jit(solution)/shard_map/ppermute | solution.py:31
  106.2 3.9 collective-permute-start.35
  165.0 38.3 %copy-start.5 = (bf16[384,1152]{1,0:T(8,128)(2,1)S(1)}, bf16[384,1152]{1,0:T(8,128)(2,1)}, u32[]{:S(2)}) copy-start(bf16[384,1152]{1,0:T(8,128)(2,1)} %weight.3) | copy-start | bytes 2654212
  210.8 4.0 collective-permute-start.36
  213.2 4.5 %collective-permute-start.37 = (bf16[64,384]{1,0:T(8,128)(2,1)S(1)}, bf16[64,384]{1,0:T(8,128)(2,1)S(1)}, u32[]{:S(2)}, u32[]{:S(2)}) collective-permute-start(bf16[64,384]{1,0:T(8,128)(2,1)S(1)} %get-tuple-element.256), channel_id=1, source_target_pairs={{0,2},{1,3},{2,0},{3,1},{4,6},{5,7},{6,4},{7,5},{8,10},{9,11},{10,... | collective-permute-start | bytes 147464 | tf_op jit(solution)/shard_map/ppermute | solution.py:31
  213.8 4.4 collective-permute-start.38
  230.4 6.5 %collective-permute-start.39 = (bf16[256,192]{1,0:T(8,128)(2,1)S(1)}, bf16[256,192]{1,0:T(8,128)(2,1)S(1)}, u32[]{:S(2)}, u32[]{:S(2)}) collective-permute-start(bf16[256,192]{1,0:T(8,128)(2,1)S(1)} %get-tuple-element.268), channel_id=1, source_target_pairs={{0,1},{1,2},{2,3},{3,0},{4,5},{5,6},{6,7},{7,4},{8,9},{9,10},{10,1... | collective-permute-start | bytes 294920 | tf_op jit(solution)/shard_map/ppermute | solution.py:31
  230.4 6.4 %collective-permute-start.40 = (bf16[256,192]{1,0:T(8,128)(2,1)S(1)}, bf16[256,192]{1,0:T(8,128)(2,1)S(1)}, u32[]{:S(2)}, u32[]{:S(2)}) collective-permute-start(bf16[256,192]{1,0:T(8,128)(2,1)S(1)} %get-tuple-element.269), channel_id=1, source_target_pairs={{0,2},{1,3},{2,0},{3,1},{4,6},{5,7},{6,4},{7,5},{8,10},{9,11},{10,... | collective-permute-start | bytes 294920 | tf_op jit(solution)/shard_map/ppermute | solution.py:31
  231.9 5.6 %collective-permute-start.41 = (bf16[256,192]{1,0:T(8,128)(2,1)S(1)}, bf16[256,192]{1,0:T(8,128)(2,1)S(1)}, u32[]{:S(2)}, u32[]{:S(2)}) collective-permute-start(bf16[256,192]{1,0:T(8,128)(2,1)S(1)} %get-tuple-element.270), channel_id=1, source_target_pairs={{0,3},{1,0},{2,1},{3,2},{4,7},{5,4},{6,5},{7,6},{8,11},{9,8},{10,9... | collective-permute-start | bytes 294920 | tf_op jit(solution)/shard_map/ppermute | solution.py:31
  254.0 5.2 %collective-permute-start.2 = (f32[112,128]{1,0:T(8,128)S(1)}, f32[112,128]{1,0:T(8,128)S(1)}, u32[]{:S(2)}, u32[]{:S(2)}) collective-permute-start(f32[112,128]{1,0:T(8,128)S(1)} %bitcast.55), channel_id=1, source_target_pairs={{0,3},{1,0},{2,1},{3,2},{4,7},{5,4},{6,5},{7,6},{8,11},{9,8},{10,9... | collective-permute-start | bytes 172040 | tf_op jit(solution)/shard_map/cond/branch_1_fun/ppermute | solution.py:31
  256.4 5.1 %collective-permute-start.1 = (f32[112,128]{1,0:T(8,128)S(1)}, f32[112,128]{1,0:T(8,128)S(1)}, u32[]{:S(2)}, u32[]{:S(2)}) collective-permute-start(f32[112,128]{1,0:T(8,128)S(1)} %bitcast.56), channel_id=1, source_target_pairs={{0,2},{1,3},{2,0},{3,1},{4,6},{5,7},{6,4},{7,5},{8,10},{9,11},{10,... | collective-permute-start | bytes 172040 | tf_op jit(solution)/shard_map/cond/branch_1_fun/ppermute | solution.py:31
  256.4 5.8 %collective-permute-start = (f32[112,128]{1,0:T(8,128)S(1)}, f32[112,128]{1,0:T(8,128)}, u32[]{:S(2)}, u32[]{:S(2)}) collective-permute-start(f32[112,128]{1,0:T(8,128)S(1)} %bitcast.57), channel_id=1, source_target_pairs={{0,1},{1,2},{2,3},{3,0},{4,5},{5,6},{6,7},{7,4},{8,9},{9,10},{10,1... | collective-permute-start | bytes 172040 | tf_op jit(solution)/shard_map/cond/branch_1_fun/ppermute | solution.py:31
  263.5 8.5 %collective-permute-start.3 = (bf16[384,640]{1,0:T(8,128)(2,1)S(1)}, bf16[384,640]{1,0:T(8,128)(2,1)S(1)}, u32[]{:S(2)}, u32[]{:S(2)}) collective-permute-start(bf16[384,640]{1,0:T(8,128)(2,1)S(1)} %pad_maximum_fusion), channel_id=1, source_target_pairs={{0,4},{4,0},{1,5},{5,1},{2,6},{6,2},{3,7},{7,3},{8,12},{12,8},{9,1... | collective-permute-start | bytes 1474568 | tf_op jit(solution)/shard_map/cond/branch_1_fun/ppermute | solution.py:35
  272.2 91.1 %copy-start.36 = (f32[1,14208]{1,0:T(1,128)S(1)}, f32[1,14208]{1,0:T(1,128)}, u32[]{:S(2)}) copy-start(f32[1,14208]{1,0:T(1,128)} %copy-done.35) | copy-start | bytes 170500 | tf_op jit(solution)/shard_map/cond
  272.2 7.6 %collective-permute-start.4 = (bf16[96,640]{1,0:T(8,128)(2,1)S(1)}, bf16[96,640]{1,0:T(8,128)(2,1)S(1)}, u32[]{:S(2)}, u32[]{:S(2)}) collective-permute-start(bf16[96,640]{1,0:T(8,128)(2,1)S(1)} %get-tuple-element.391), channel_id=1, source_target_pairs={{0,16},{8,24},{16,0},{24,8},{1,17},{9,25},{17,1},{25,9},{2,18},{10... | collective-permute-start | bytes 368648 | tf_op jit(solution)/shard_map/cond/branch_1_fun/ppermute | solution.py:31
  275.0 7.4 %collective-permute-start.6 = (bf16[96,640]{1,0:T(8,128)(2,1)S(1)}, bf16[96,640]{1,0:T(8,128)(2,1)S(1)}, u32[]{:S(2)}, u32[]{:S(2)}) collective-permute-start(bf16[96,640]{1,0:T(8,128)(2,1)S(1)} %get-tuple-element.392), channel_id=1, source_target_pairs={{0,24},{8,0},{16,8},{24,16},{1,25},{9,1},{17,9},{25,17},{2,26},{10... | collective-permute-start | bytes 368648 | tf_op jit(solution)/shard_map/cond/branch_1_fun/ppermute | solution.py:31
  275.9 7.3 %collective-permute-start.5 = (bf16[96,640]{1,0:T(8,128)(2,1)S(1)}, bf16[96,640]{1,0:T(8,128)(2,1)S(1)}, u32[]{:S(2)}, u32[]{:S(2)}) collective-permute-start(bf16[96,640]{1,0:T(8,128)(2,1)S(1)} %get-tuple-element.393), channel_id=1, source_target_pairs={{0,8},{8,16},{16,24},{24,0},{1,9},{9,17},{17,25},{25,1},{2,10},{10... | collective-permute-start | bytes 368648 | tf_op jit(solution)/shard_map/cond/branch_1_fun/ppermute | solution.py:31
  283.2 4.3 collective-permute-start.7
  286.0 3.1 collective-permute-start.9
  286.8 4.0 collective-permute-start.8
  290.7 3.2 collective-permute-start.12
  290.8 4.3 collective-permute-start.11
  292.5 4.0 collective-permute-start.10
  296.5 9.3 %collective-permute-start.15 = (bf16[96,640]{1,0:T(8,128)(2,1)S(1)}, bf16[96,640]{1,0:T(8,128)(2,1)S(1)}, u32[]{:S(2)}, u32[]{:S(2)}) collective-permute-start(bf16[96,640]{1,0:T(8,128)(2,1)S(1)} %pad_maximum_fusion.1), channel_id=1, source_target_pairs={{0,24},{8,0},{16,8},{24,16},{1,25},{9,1},{17,9},{25,17},{2,26},{10... | collective-permute-start | bytes 368648 | tf_op jit(solution)/shard_map/cond/branch_1_fun/ppermute | solution.py:31
  297.9 7.9 %collective-permute-start.14 = (bf16[96,640]{1,0:T(8,128)(2,1)S(1)}, bf16[96,640]{1,0:T(8,128)(2,1)S(1)}, u32[]{:S(2)}, u32[]{:S(2)}) collective-permute-start(bf16[96,640]{1,0:T(8,128)(2,1)S(1)} %pad_maximum_fusion.1), channel_id=1, source_target_pairs={{0,16},{8,24},{16,0},{24,8},{1,17},{9,25},{17,1},{25,9},{2,18},{10... | collective-permute-start | bytes 368648 | tf_op jit(solution)/shard_map/cond/branch_1_fun/ppermute | solution.py:31
  298.5 7.2 %collective-permute-start.13 = (bf16[96,640]{1,0:T(8,128)(2,1)S(1)}, bf16[96,640]{1,0:T(8,128)(2,1)S(1)}, u32[]{:S(2)}, u32[]{:S(2)}) collective-permute-start(bf16[96,640]{1,0:T(8,128)(2,1)S(1)} %pad_maximum_fusion.1), channel_id=1, source_target_pairs={{0,8},{8,16},{16,24},{24,0},{1,9},{9,17},{17,25},{25,1},{2,10},{10... | collective-permute-start | bytes 368648 | tf_op jit(solution)/shard_map/cond/branch_1_fun/ppermute | solution.py:31
  305.8 39.4 %collective-permute-start.18 = (bf16[384,640]{1,0:T(8,128)(2,1)S(1)}, bf16[384,640]{1,0:T(8,128)(2,1)S(1)}, u32[]{:S(2)}, u32[]{:S(2)}) collective-permute-start(bf16[384,640]{1,0:T(8,128)(2,1)S(1)} %constant_dynamic-update-slice_fusion.19.refs_0_), channel_id=1, source_target_pairs={{0,3},{1,0},{2,1},{3,2},{4,7},{5,4},{6,5},{7,6},{8,11},{9,8},{10,9... | collective-permute-start | bytes 1474568 | tf_op jit(solution)/shard_map/cond/branch_1_fun/ppermute | solution.py:31
  307.3 37.9 %collective-permute-start.17 = (bf16[384,640]{1,0:T(8,128)(2,1)S(1)}, bf16[384,640]{1,0:T(8,128)(2,1)S(1)}, u32[]{:S(2)}, u32[]{:S(2)}) collective-permute-start(bf16[384,640]{1,0:T(8,128)(2,1)S(1)} %constant_dynamic-update-slice_fusion.19.refs_0_), channel_id=1, source_target_pairs={{0,2},{1,3},{2,0},{3,1},{4,6},{5,7},{6,4},{7,5},{8,10},{9,11},{10,... | collective-permute-start | bytes 1474568 | tf_op jit(solution)/shard_map/cond/branch_1_fun/ppermute | solution.py:31
  308.7 37.0 %collective-permute-start.16 = (bf16[384,640]{1,0:T(8,128)(2,1)S(1)}, bf16[384,640]{1,0:T(8,128)(2,1)S(1)}, u32[]{:S(2)}, u32[]{:S(2)}) collective-permute-start(bf16[384,640]{1,0:T(8,128)(2,1)S(1)} %constant_dynamic-update-slice_fusion.19.refs_0_), channel_id=1, source_target_pairs={{0,1},{1,2},{2,3},{3,0},{4,5},{5,6},{6,7},{7,4},{8,9},{9,10},{10,1... | collective-permute-start | bytes 1474568 | tf_op jit(solution)/shard_map/cond/branch_1_fun/ppermute | solution.py:31
  308.8 25.8 %collective-permute-start.23 = (bf16[256,768]{1,0:T(8,128)(2,1)S(1)}, bf16[256,768]{1,0:T(8,128)(2,1)S(1)}, u32[]{:S(2)}, u32[]{:S(2)}) collective-permute-start(bf16[256,768]{1,0:T(8,128)(2,1)S(1)} %get-tuple-element.124), channel_id=1, source_target_pairs={{0,3},{1,0},{2,1},{3,2},{4,7},{5,4},{6,5},{7,6},{8,11},{9,8},{10,9... | collective-permute-start | bytes 1179656 | tf_op jit(solution)/shard_map/cond/branch_1_fun/ppermute | solution.py:31
  311.4 34.4 %collective-permute-start.24 = (bf16[256,768]{1,0:T(8,128)(2,1)}, bf16[256,768]{1,0:T(8,128)(2,1)S(1)}, u32[]{:S(2)}, u32[]{:S(2)}) collective-permute-start(bf16[256,768]{1,0:T(8,128)(2,1)} %get-tuple-element.125), channel_id=1, source_target_pairs={{0,2},{1,3},{2,0},{3,1},{4,6},{5,7},{6,4},{7,5},{8,10},{9,11},{10,... | collective-permute-start | bytes 1179656 | tf_op jit(solution)/shard_map/cond/branch_1_fun/ppermute | solution.py:31
  335.3 32.8 %collective-permute-start.19 = (bf16[384,640]{1,0:T(8,128)(2,1)S(1)}, bf16[384,640]{1,0:T(8,128)(2,1)S(1)}, u32[]{:S(2)}, u32[]{:S(2)}) collective-permute-start(bf16[384,640]{1,0:T(8,128)(2,1)S(1)} %constant_dynamic-update-slice_fusion.19.refs_0_), channel_id=1, source_target_pairs={{0,4},{4,0},{1,5},{5,1},{2,6},{6,2},{3,7},{7,3},{8,12},{12,8},{9,1... | collective-permute-start | bytes 1474568 | tf_op jit(solution)/shard_map/cond/branch_1_fun/ppermute | solution.py:35
  345.3 22.9 %collective-permute-start.22 = (bf16[384,640]{1,0:T(8,128)(2,1)S(1)}, bf16[384,640]{1,0:T(8,128)(2,1)}, u32[]{:S(2)}, u32[]{:S(2)}) collective-permute-start(bf16[384,640]{1,0:T(8,128)(2,1)S(1)} %collective-permute-done.18.refs_3_), channel_id=1, source_target_pairs={{0,4},{4,0},{1,5},{5,1},{2,6},{6,2},{3,7},{7,3},{8,12},{12,8},{9,1... | collective-permute-start | bytes 1474568 | tf_op jit(solution)/shard_map/cond/branch_1_fun/ppermute | solution.py:35
  345.3 22.9 %collective-permute-start.21 = (bf16[384,640]{1,0:T(8,128)(2,1)S(1)}, bf16[384,640]{1,0:T(8,128)(2,1)}, u32[]{:S(2)}, u32[]{:S(2)}) collective-permute-start(bf16[384,640]{1,0:T(8,128)(2,1)S(1)} %collective-permute-done.17.refs_2_), channel_id=1, source_target_pairs={{0,4},{4,0},{1,5},{5,1},{2,6},{6,2},{3,7},{7,3},{8,12},{12,8},{9,1... | collective-permute-start | bytes 1474568 | tf_op jit(solution)/shard_map/cond/branch_1_fun/ppermute | solution.py:35
  345.8 22.4 %collective-permute-start.20 = (bf16[384,640]{1,0:T(8,128)(2,1)S(1)}, bf16[384,640]{1,0:T(8,128)(2,1)}, u32[]{:S(2)}, u32[]{:S(2)}) collective-permute-start(bf16[384,640]{1,0:T(8,128)(2,1)S(1)} %collective-permute-done.16.refs_1_), channel_id=1, source_target_pairs={{0,4},{4,0},{1,5},{5,1},{2,6},{6,2},{3,7},{7,3},{8,12},{12,8},{9,1... | collective-permute-start | bytes 1474568 | tf_op jit(solution)/shard_map/cond/branch_1_fun/ppermute | solution.py:35
  346.6 16.6 %collective-permute-start.25 = (bf16[256,768]{1,0:T(8,128)(2,1)}, bf16[256,768]{1,0:T(8,128)(2,1)}, u32[]{:S(2)}, u32[]{:S(2)}) collective-permute-start(bf16[256,768]{1,0:T(8,128)(2,1)} %copy-done.22), channel_id=1, source_target_pairs={{0,1},{1,2},{2,3},{3,0},{4,5},{5,6},{6,7},{7,4},{8,9},{9,10},{10,1... | collective-permute-start | bytes 1179656 | tf_op jit(solution)/shard_map/cond/branch_1_fun/ppermute | solution.py:31
  (82 other events, 824.5 us)
Sparse Core Ops, SparseCore 0:
  13.1 75.3 all-gather.1
  230.5 189.3 all-reduce.4
